TPU v7x, 128 devices: a whole 4x4x4 slice. The times are simulated.
128 devices in a mesh: seq: 8 (over x, core), dp: 16 (over z, y).
Axes of the slice: x: 4, y: 4, z: 4, core: 2. Of those that a mesh axis runs over, the one named last changes fastest.
Arguments:
- tokens: bfloat16 [4, 16, 64, 128, 256], P(None, 'dp', 'seq'), may hold values from -6 to 6
- lengths: int32 [4, 16, 64], P(None, 'dp'), may hold values from 1 to 64, as said below
- visible: int32 [4, 16, 64, 128], P(None, 'dp'), may hold values from 0 to 1, as said below
- norm_gains: bfloat16 [2, 256], P(None, ('seq', 'dp')), may hold values from 0.5 to 1.5
- norm_biases: bfloat16 [2, 256], P(None, ('seq', 'dp')), may hold values from -1.25 to 1.25
- w_qkv: bfloat16 [256, 768], P(('seq', 'dp')), may hold values from -0.5 to 0.5
- w_out: bfloat16 [256, 256], P(('seq', 'dp')), may hold values from -1.5 to 1.5
- w_up: bfloat16 [256, 1024], P(('seq', 'dp')), may hold values from -0.375 to 0.375
- w_down: bfloat16 [1024, 256], P(('seq', 'dp')), may hold values from -0.1875 to 0.1875
- proj_biases: bfloat16 [4, 256], P(None, ('seq', 'dp')), may hold values from -1.25 to 1.25
- up_bias: bfloat16 [1024], P(('seq', 'dp')), may hold values from -1.25 to 1.25
- mask_token: bfloat16 [256], P(('seq', 'dp')), may hold values from -6 to 6
- time_embed: bfloat16 [64, 256], P(None, ('seq', 'dp')), may hold values from -3 to 3
- dec_grad: bfloat16 [4, 16, 64, 128, 256], P(None, 'dp', None, 'seq'), may hold values from -6 to 6
Outputs:
- decoded: bfloat16 [4, 16, 64, 128, 256], P(None, 'dp', None, 'seq')
- grad_tokens: float32 [4, 16, 64, 128, 256], P(None, 'dp', 'seq')
- grad_norm_gains: float32 [2, 256], P(None, ('seq', 'dp'))
- grad_norm_biases: float32 [2, 256], P(None, ('seq', 'dp'))
- grad_w_qkv: float32 [256, 768], P(('seq', 'dp'))
- grad_w_out: float32 [256, 256], P(('seq', 'dp'))
- grad_w_up: float32 [256, 1024], P(('seq', 'dp'))
- grad_w_down: float32 [1024, 256], P(('seq', 'dp'))
- grad_proj_biases: float32 [4, 256], P(None, ('seq', 'dp'))
- grad_up_bias: float32 [1024], P(('seq', 'dp'))
- grad_mask_token: float32 [256], P(('seq', 'dp'))
- grad_time_embed: float32 [64, 256], P(None, ('seq', 'dp'))
Inputs may be any that keep to these rules, and one draw needn't show every extreme that they name: `lengths`: in every micro-batch and batch one trajectory has all 64 timesteps. `visible`: slot 0 of every trajectory is 1.
All inputs are finite; a program needn't handle non-finite values.
Results may differ from a plain program's by a relative error of at most 0.015.
Values may be sent and summed in bfloat16 or wider, within the bound.
A program may use at most 192 MiB of HBM per device.

v0:
```python
import jax
import jax.numpy as jnp
from jax import lax
from jax.sharding import Mesh
from jax.sharding import PartitionSpec as P

HEADS = 4
SEQ_DP = ("seq_0", "seq_1", "dp_0", "dp_1")
SEQ = ("seq_0", "seq_1")
DP = ("dp_0", "dp_1")


NORM_EPS = 1e-05


def sent_together(arrays, axis, dim, along):
    ends, at = ([], 0)
    for a in arrays[:-1]:
        at += a.shape[along]
        ends.append(at)
    both = jnp.concatenate(arrays, axis=along)
    return tuple(jnp.split(lax.all_gather(both, axis, axis=dim, tiled=True), ends, axis=along))


def in_blocks(array, dim, devices):
    dims = array.shape
    parts = array.reshape(*dims[:dim], devices, dims[dim] // devices, *dims[dim + 1 :])
    return jnp.moveaxis(parts, dim, 0)


def summed_on_arrival(array, axis, dim):
    parts = in_blocks(array, dim, lax.axis_size(axis))
    arrived = lax.all_to_all(parts, axis, split_axis=0, concat_axis=0, tiled=True)
    return arrived.sum(axis=0)


def summed_rows(array, axes, dim):
    far, near = axes
    own = summed_on_arrival(in_blocks(array, dim, lax.axis_size(far)), near, dim + 1)
    return jnp.sum(lax.all_to_all(own, far, 0, 0, tiled=True), axis=0)


def in_one_piece(arrays, axis, dim, along):
    ends, at = ([], 0)
    for a in arrays[:-1]:
        at += a.shape[along]
        ends.append(at)
    both = jnp.concatenate(arrays, axis=along)
    return tuple(jnp.split(summed_rows(both, axis, dim), ends, axis=along))


def layer_norm(values_in, gain_row, shift_row):
    centre = values_in - jnp.mean(values_in, axis=-1, keepdims=True)
    spread = jnp.mean(centre * centre, axis=-1, keepdims=True)
    return centre * lax.rsqrt(spread + NORM_EPS) * gain_row + shift_row


def gelu_tanh(values_in):
    return jax.nn.gelu(values_in, approximate=True)


def fetch_weights(
    norm_gains,
    norm_biases,
    w_qkv,
    w_out,
    w_up,
    w_down,
    proj_biases,
    up_bias,
    mask_token,
    time_embed,
):
    return (
        *sent_together((norm_gains, norm_biases), SEQ_DP, 1, 0),
        *sent_together((w_qkv, w_out, w_up), SEQ_DP, 0, 1),
        lax.all_gather(w_down, SEQ_DP, axis=0, tiled=True),
        lax.all_gather(proj_biases, SEQ_DP, axis=1, tiled=True),
        lax.all_gather(up_bias, SEQ_DP, axis=0, tiled=True),
        lax.all_gather(mask_token, SEQ_DP, axis=0, tiled=True),
        lax.all_gather(time_embed, SEQ_DP, axis=1, tiled=True),
    )


def reduce_grads(grads):
    return (
        *in_one_piece((grads[0], grads[1]), (("seq_0", "seq_1", "dp_0"), "dp_1"), 1, 0),
        *in_one_piece((grads[2], grads[3], grads[4]), (("seq_0", "seq_1", "dp_0"), "dp_1"), 0, 1),
        summed_rows(grads[5], (("seq_0", "seq_1", "dp_0"), "dp_1"), 0),
        summed_rows(grads[6], (("seq_0", "seq_1", "dp_0"), "dp_1"), 1),
        summed_rows(grads[7], (("seq_0", "seq_1", "dp_0"), "dp_1"), 0),
        summed_rows(grads[8], (("seq_0", "seq_1", "dp_0"), "dp_1"), 0),
        summed_rows(grads[9], (("seq_0", "seq_1", "dp_0"), "dp_1"), 1),
    )


def accumulate(running, fresh_terms):
    if running is None:
        return fresh_terms
    return tuple((earlier + latest for earlier, latest in zip(running, fresh_terms)))


def per_device(
    tokens,
    lengths,
    visible,
    norm_gains,
    norm_biases,
    w_qkv,
    w_out,
    w_up,
    w_down,
    proj_biases,
    up_bias,
    mask_token,
    time_embed,
    dec_grad,
):
    micro_count, _unused, traj_share, slot_count, model_width = tokens.shape
    group_size = lax.axis_size(SEQ)
    traj_count = traj_share * group_size
    part_slots = slot_count // group_size
    head_size = model_width // HEADS
    score_scale = head_size ** (-0.5)
    seq_index = lax.axis_index(SEQ)
    slot_index = jnp.arange(slot_count, dtype=jnp.int32)
    first_traj = seq_index * traj_share
    first_slot = seq_index * part_slots
    slot_mine = first_slot + jnp.arange(part_slots, dtype=jnp.int32)
    f32 = jnp.float32
    low_type = jnp.bfloat16
    kept_weights = fetch_weights(
        norm_gains,
        norm_biases,
        w_qkv,
        w_out,
        w_up,
        w_down,
        proj_biases,
        up_bias,
        mask_token,
        time_embed,
    )
    grad_totals = None
    dec_parts = []
    input_grads = []
    for micro_step in range(micro_count):
        (
            gains_all,
            shifts_all,
            weight_qkv,
            weight_out,
            weight_up,
            weight_down,
            biases_all,
            bias_up,
            token_mask,
            step_embed,
        ) = kept_weights
        gains_f = gains_all.astype(f32)
        shifts_f = shifts_all.astype(f32)
        biases_f = biases_all.astype(f32)
        inputs_now = tokens[micro_step, 0].astype(f32)
        length_now = lengths[micro_step, 0]
        shown_now = visible[micro_step, 0] > 0
        length_enc = lax.dynamic_slice_in_dim(length_now, first_traj, traj_share, 0)
        shown_enc = lax.dynamic_slice_in_dim(shown_now, first_traj, traj_share, 0)
        valid_enc = slot_index[None, :] // 2 < length_enc[:, None]
        key_open = valid_enc & shown_enc
        normed_first, first_back = jax.vjp(layer_norm, inputs_now, gains_f[0], shifts_f[0])
        normed_first_low = normed_first.astype(low_type)
        qkv_bias = jnp.concatenate([biases_f[0], jnp.zeros_like(biases_f[0]), biases_f[1]])
        qkv_rows = (
            jnp.dot(normed_first_low, weight_qkv, preferred_element_type=f32) + qkv_bias
        ).astype(low_type)
        head_shape = (traj_share, slot_count, HEADS, head_size)
        query_rows = qkv_rows[..., :model_width].reshape(head_shape)
        key_rows = qkv_rows[..., model_width : 2 * model_width].reshape(head_shape)
        value_rows = qkv_rows[..., 2 * model_width :].reshape(head_shape)

        def masked_scores():
            raw_scores = (
                jnp.einsum("tqhd,tkhd->thqk", query_rows, key_rows, preferred_element_type=f32)
                * score_scale
            )
            return jnp.where(key_open[:, None, None, :], raw_scores, -1e30)

        scores = masked_scores()
        row_max = jnp.max(scores, axis=-1, keepdims=True)
        shifted = jnp.exp(scores - row_max)
        row_total = jnp.sum(shifted, axis=-1, keepdims=True)
        log_total = row_max + jnp.log(row_total)
        probs_low = (shifted / row_total).astype(low_type)
        attended = jnp.einsum("thqk,tkhd->tqhd", probs_low, value_rows, preferred_element_type=f32)
        attended_low = attended.reshape(traj_share, slot_count, model_width).astype(low_type)
        mixed_rows = (
            inputs_now + jnp.dot(attended_low, weight_out, preferred_element_type=f32) + biases_f[2]
        )
        normed_second, second_back = jax.vjp(layer_norm, mixed_rows, gains_f[1], shifts_f[1])
        normed_second_low = normed_second.astype(low_type)
        hidden_pre = jnp.dot(
            normed_second_low, weight_up, preferred_element_type=f32
        ) + bias_up.astype(f32)
        hidden_act, gelu_back = jax.vjp(gelu_tanh, hidden_pre)
        hidden_low = hidden_act.astype(low_type)
        encoded = (
            mixed_rows + jnp.dot(hidden_low, weight_down, preferred_element_type=f32) + biases_f[3]
        )
        encoded_low = encoded.astype(low_type)
        arrived = lax.all_to_all(encoded_low, SEQ, split_axis=1, concat_axis=0, tiled=True)
        shown_dec = lax.dynamic_slice_in_dim(shown_now, first_slot, part_slots, 1)
        valid_dec = slot_mine[None, :] // 2 < length_now[:, None]
        step_rows = lax.dynamic_slice_in_dim(
            jnp.repeat(step_embed.astype(f32), 2, axis=0), first_slot, part_slots, 0
        )
        chosen = jnp.where(
            shown_dec[..., None], arrived.astype(f32), token_mask.astype(f32)[None, None, :]
        )
        decoded_now = jnp.where(valid_dec[..., None], chosen + step_rows[None], 0.0).astype(
            low_type
        )
        dec_parts.append(decoded_now[None, None])
        grad_dec_now = dec_grad[micro_step, 0].astype(f32)
        live_rows = valid_dec[..., None]
        grad_token_mask = jnp.sum(
            jnp.where(live_rows & ~shown_dec[..., None], grad_dec_now, 0.0), axis=(0, 1)
        )
        grad_steps_mine = jnp.sum(
            jnp.where(live_rows, grad_dec_now, 0.0).reshape(
                traj_count, part_slots // 2, 2, model_width
            ),
            axis=(0, 2),
        )
        grad_steps = lax.dynamic_update_slice_in_dim(
            jnp.zeros((slot_count // 2, model_width), f32), grad_steps_mine, first_slot // 2, 0
        )
        back_send = jnp.where(live_rows & shown_dec[..., None], grad_dec_now, 0.0).astype(low_type)
        grad_encoded_low = lax.all_to_all(back_send, SEQ, split_axis=0, concat_axis=1, tiled=True)
        grad_encoded = grad_encoded_low.astype(f32)
        grad_weight_down = jnp.einsum(
            "tpf,tpd->fd", hidden_low, grad_encoded_low, preferred_element_type=f32
        )
        grad_bias_down = jnp.sum(grad_encoded, axis=(0, 1))
        grad_hidden_act = jnp.einsum(
            "tpd,fd->tpf", grad_encoded_low, weight_down, preferred_element_type=f32
        )
        grad_hidden_pre = gelu_back(grad_hidden_act)[0].astype(low_type)
        grad_bias_up = jnp.sum(grad_hidden_pre.astype(f32), axis=(0, 1))
        grad_weight_up = jnp.einsum(
            "tpd,tpf->df", normed_second_low, grad_hidden_pre, preferred_element_type=f32
        )
        grad_normed_second = jnp.einsum(
            "tpf,df->tpd", grad_hidden_pre, weight_up, preferred_element_type=f32
        )
        grad_mixed_norm, grad_gain_second, grad_shift_second = second_back(grad_normed_second)
        grad_mixed = grad_encoded + grad_mixed_norm
        grad_attn_low = grad_mixed.astype(low_type)
        grad_weight_out = jnp.einsum(
            "tpd,tpe->de", attended_low, grad_attn_low, preferred_element_type=f32
        )
        grad_bias_out = jnp.sum(grad_attn_low.astype(f32), axis=(0, 1))
        grad_attended = jnp.einsum(
            "tpe,de->tpd", grad_attn_low, weight_out, preferred_element_type=f32
        )
        grad_attended_low = grad_attended.astype(low_type).reshape(head_shape)
        probs_again = jnp.exp(masked_scores() - log_total)
        grad_values = jnp.einsum(
            "thqk,tqhd->tkhd",
            probs_again.astype(low_type),
            grad_attended_low,
            preferred_element_type=f32,
        )
        grad_probs = jnp.einsum(
            "tqhd,tkhd->thqk", grad_attended_low, value_rows, preferred_element_type=f32
        )
        row_inner = jnp.sum(probs_again * grad_probs, axis=-1, keepdims=True)
        grad_scores_low = (probs_again * (grad_probs - row_inner)).astype(low_type)
        grad_queries = (
            jnp.einsum("thqk,tkhd->tqhd", grad_scores_low, key_rows, preferred_element_type=f32)
            * score_scale
        )
        grad_keys = (
            jnp.einsum("thqk,tqhd->tkhd", grad_scores_low, query_rows, preferred_element_type=f32)
            * score_scale
        )
        flat_shape = (traj_share, slot_count, model_width)
        grad_qkv_low = jnp.concatenate(
            [
                grad_queries.reshape(flat_shape),
                grad_keys.reshape(flat_shape),
                grad_values.reshape(flat_shape),
            ],
            axis=-1,
        ).astype(low_type)
        grad_qkv_sums = jnp.sum(grad_qkv_low.astype(f32), axis=(0, 1))
        grad_weight_qkv = jnp.einsum(
            "tpd,tpn->dn", normed_first_low, grad_qkv_low, preferred_element_type=f32
        )
        grad_normed_first = jnp.einsum(
            "tpn,dn->tpd", grad_qkv_low, weight_qkv, preferred_element_type=f32
        )
        grad_input_norm, grad_gain_first, grad_shift_first = first_back(grad_normed_first)
        input_grads.append((grad_mixed + grad_input_norm)[None, None])
        step_grads = (
            jnp.stack([grad_gain_first, grad_gain_second]),
            jnp.stack([grad_shift_first, grad_shift_second]),
            grad_weight_qkv,
            grad_weight_out,
            grad_weight_up,
            grad_weight_down,
            jnp.stack(
                [
                    grad_qkv_sums[:model_width],
                    grad_qkv_sums[2 * model_width :],
                    grad_bias_out,
                    grad_bias_down,
                ]
            ),
            grad_bias_up,
            grad_token_mask,
            grad_steps,
        )
        grad_totals = accumulate(grad_totals, step_grads)
    grad_totals = reduce_grads(grad_totals)
    return (
        jnp.concatenate(dec_parts, axis=0),
        jnp.concatenate(input_grads, axis=0),
        grad_totals[0],
        grad_totals[1],
        grad_totals[2],
        grad_totals[3],
        grad_totals[4],
        grad_totals[5],
        grad_totals[6],
        grad_totals[7],
        grad_totals[8],
        grad_totals[9],
    )


def solution(mesh):
    finer = Mesh(mesh.devices.reshape(4, 2, 4, 4), ("seq_0", "seq_1", "dp_0", "dp_1"))
    return jax.shard_map(
        per_device,
        mesh=finer,
        in_specs=(
            P(None, DP, SEQ, None, None),
            P(None, DP, None),
            P(None, DP, None, None),
            P(None, SEQ_DP),
            P(None, SEQ_DP),
            P(SEQ_DP, None),
            P(SEQ_DP, None),
            P(SEQ_DP, None),
            P(SEQ_DP, None),
            P(None, SEQ_DP),
            P(SEQ_DP),
            P(SEQ_DP),
            P(None, SEQ_DP),
            P(None, DP, None, SEQ, None),
        ),
        out_specs=(
            P(None, DP, None, SEQ, None),
            P(None, DP, SEQ, None, None),
            P(None, SEQ_DP),
            P(None, SEQ_DP),
            P(SEQ_DP, None),
            P(SEQ_DP, None),
            P(SEQ_DP, None),
            P(SEQ_DP, None),
            P(None, SEQ_DP),
            P(SEQ_DP),
            P(SEQ_DP),
            P(None, SEQ_DP),
        ),
        check_vma=False,
    )
```

profile of v0, /device:TPU:0, one launch (start us, length us, event | category | flops | bytes accessed | tf_op | source)
XLA Modules:
  0.0 804.4 jit_solution(7384295804269305045)
XLA Ops:
  11.8 4.6 fusion.128
  17.2 4.5 all-to-all-start.18
  22.5 48.9 %all-gather.2 = bf16[128,2,4]{2,1,0:T(2,128)(2,1)S(1)} all-gather(bf16[1,2,4]{2,1,0:T(2,128)(2,1)S(1)} %bitcast.807), channel_id=1, replica_groups=mesh['seq_0'=4,'seq_1'=2,'dp_0'=4,'dp_1'=4] {'seq_0','seq_1','dp_0','dp_1'}, dimensions={0}, use_global_device_ids=true | all-gather | bytes 2064 | tf_op jit(solution)/shard_map/all_gather | solution.py:78
  72.1 42.8 %all-gather.3 = bf16[128,2,64]{2,1,0:T(2,128)(2,1)S(1)} all-gather(bf16[1,2,64]{2,1,0:T(2,128)(2,1)S(1)} %bitcast.808), channel_id=1, replica_groups=mesh['seq_0'=4,'seq_1'=2,'dp_0'=4,'dp_1'=4] {'seq_0','seq_1','dp_0','dp_1'}, dimensions={0}, use_global_device_ids=true | all-gather | bytes 33024 | tf_op jit(solution)/shard_map/all_gather | solution.py:81
  115.7 44.2 %all-gather = bf16[128,2,4]{2,1,0:T(2,128)(2,1)S(1)} all-gather(bf16[1,2,4]{2,1,0:T(2,128)(2,1)S(1)} %bitcast.809), channel_id=1, replica_groups=mesh['seq_0'=4,'seq_1'=2,'dp_0'=4,'dp_1'=4] {'seq_0','seq_1','dp_0','dp_1'}, dimensions={0}, use_global_device_ids=true | all-gather | bytes 2064 | tf_op jit(solution)/shard_map/all_gather | solution.py:22
  160.1 3.5 all-to-all-start.5
  164.1 9.8 %all-to-all-done.5 = bf16[64,16,256]{2,1,0:T(8,128)(2,1)S(1)} async-done(((bf16[64,16,256]{2,1,0:T(8,128)(2,1)}), bf16[64,16,256]{2,1,0:T(8,128)(2,1)S(1)}, u32[]{:S(2)}, u32[]{:S(2)}) %all-to-all-start.5) | async-done | bytes 524320 | tf_op jit(solution)/shard_map/all_to_all | solution.py:238
  173.9 3.5 all-to-all-start.4
  177.5 10.2 %all-to-all-done.4 = bf16[64,16,256]{2,1,0:T(8,128)(2,1)S(1)} async-done(((bf16[64,16,256]{2,1,0:T(8,128)(2,1)}), bf16[64,16,256]{2,1,0:T(8,128)(2,1)S(1)}, u32[]{:S(2)}, u32[]{:S(2)}) %all-to-all-start.4) | async-done | bytes 524320 | tf_op jit(solution)/shard_map/all_to_all | solution.py:238
  187.6 4.1 all-to-all-start.7
  192.3 64.9 %all-reduce.2 = (bf16[1024]{0:T(1024)(128)(2,1)S(1)}, bf16[256]{0:T(256)(128)(2,1)S(1)}) all-reduce(bf16[1024]{0:T(1024)(128)(2,1)S(1)} %dynamic-update-slice.3, bf16[256]{0:T(256)(128)(2,1)S(1)} %dynamic-update-slice.4), channel_id=1, replica_groups=mesh['seq_0'=4,'seq_1'=2,'dp_0'=4,'dp_1'=4] {'seq_0','seq_1','dp_0','dp_1'}, use_global_device_ids=true, to_apply=%add | all-reduce | flops 1280 | bytes 5120
  257.8 4.2 all-to-all-start.6
  262.1 55.7 %all_gather.25 = bf16[1024,256]{1,0:T(8,128)(2,1)} all-gather(bf16[8,256]{1,0:T(8,128)(2,1)S(1)} %copy-done.180), channel_id=1, replica_groups=mesh['seq_0'=4,'seq_1'=2,'dp_0'=4,'dp_1'=4] {'seq_0','seq_1','dp_0','dp_1'}, dimensions={0}, use_global_device_ids=true | all-gather | bytes 528384 | tf_op jit(solution)/shard_map/all_gather | solution.py:77
  339.3 4.0 convert_reduce_fusion.2
  353.0 2.8 convolution_convert_fusion.6
  367.8 3.3 convolution_bitcast_fusion.10
  371.1 3.1 fusion.119
  396.8 5.0 convert_reduce_fusion.1
  401.9 6.5 multiply_convert_fusion.2
  429.1 4.0 convert_reduce_fusion.3
  441.9 4.1 convert_reduce_fusion
  449.2 4.0 fusion.219
  458.9 3.5 convolution_convert_fusion.5
  475.5 3.4 convolution_bitcast_fusion.9
  485.5 3.5 convolution_convert_fusion.7
  499.4 2.8 convolution_convert_fusion.4
  513.9 3.2 convolution_bitcast_fusion.8
  523.1 3.2 all-to-all-start.16
  537.0 4.5 fusion.112
  544.7 2.8 fusion.115
  552.7 4.8 all-to-all-start.14
  566.2 4.2 all-to-all-start
  572.6 4.0 convolution_bitcast_fusion.4
  576.5 4.1 all-to-all-done
  580.7 4.1 all-to-all-start.1
  584.9 3.8 fusion.92
  588.7 6.5 all-to-all-done.1
  595.2 4.4 all-to-all-start.2
  605.9 3.9 all-to-all-done.2
  609.9 4.1 all-to-all-start.3
  618.9 5.4 all-to-all-done.3
  624.4 4.1 all-to-all-start.19
  630.5 4.5 select_convert_fusion.3
  639.2 4.8 all-to-all-start.8
  646.1 3.2 all-to-all-done.8
  649.3 7.5 all-to-all-start.17
  663.9 3.3 all-to-all-start.20
  672.8 5.7 all-to-all-start.15
  681.6 4.2 all-to-all-done.15
  685.9 4.5 all-to-all-start.9
  691.2 6.4 all-to-all-done.9
  697.6 3.8 all-to-all-start.21
  708.7 4.2 all-to-all-start.12
  716.5 3.6 fusion.74
  721.6 3.4 reshape_reshape.8
  725.1 3.1 copy.951
  728.6 4.7 all-to-all-start.10
  734.1 4.9 add_bitcast_fusion.2
  741.1 18.6 %all-to-all-done.10 = f32[4,32,2,2048]{3,2,1,0:T(2,128)} async-done(((f32[4,32,2,2048]{3,2,1,0:T(2,128)}), f32[4,32,2,2048]{3,2,1,0:T(2,128)}, u32[]{:S(2)}, u32[]{:S(2)}) %all-to-all-start.10) | async-done | bytes 2097184 | tf_op jit(solution)/shard_map/all_to_all | solution.py:33
  759.6 5.2 all-to-all-start.13
  765.0 3.9 add_bitcast_fusion.3
  772.2 3.9 reduce_sum.1060
  776.1 7.5 all-to-all-start.11
  791.2 4.2 all-to-all-done.11
  (790 shorter events, 254.1 us)
Async XLA Ops:
  7.2 322.7 %all-gather.6.cloned.1.call-start = ((), (), s32[]{:S(2)}) async-start(), calls=%async_computation.22 | async-start | bytes 1056768 | tf_op jit(solution)/shard_map/all_gather | solution.py:22
  11.7 10.0 %copy-start.209 = (bf16[2,2]{1,0:T(2,128)(2,1)S(1)}, bf16[2,2]{1,0:T(2,128)(2,1)}, u32[]{:S(2)}) copy-start(bf16[2,2]{1,0:T(2,128)(2,1)} %param.18) | copy-start | bytes 28
  11.7 10.1 %copy-start.4 = (bf16[4,1,8,128,256]{4,3,2,1,0:T(8,128)(2,1)S(1)}, bf16[4,1,8,128,256]{4,3,2,1,0:T(8,128)(2,1)}, u32[]{:S(2)}) copy-start(bf16[4,1,8,128,256]{4,3,2,1,0:T(8,128)(2,1)} %param.14) | copy-start | bytes 6291460
  16.3 55.8 %copy-start.208 = (bf16[64,2]{0,1:T(2,128)(2,1)S(1)}, bf16[64,2]{0,1:T(2,128)(2,1)}, u32[]{:S(2)}) copy-start(bf16[64,2]{0,1:T(2,128)(2,1)} %param.26) | copy-start | bytes 772
  17.2 142.9 %all-to-all-start.18 = ((f32[4,32,2]{1,2,0:T(2,128)}), f32[4,32,2]{1,2,0:T(2,128)S(1)}, u32[]{:S(2)}, u32[]{:S(2)}) async-start(f32[4,32,2]{1,2,0:T(2,128)} %copy.876), calls=%async_computation.18 | async-start | bytes 8192 | tf_op jit(solution)/shard_map/all_to_all | solution.py:33
  115.0 76.9 %copy-start.211 = (bf16[2]{0:T(256)(128)(2,1)S(1)}, bf16[2]{0:T(256)(128)(2,1)}, u32[]{:S(2)}) copy-start(bf16[2]{0:T(256)(128)(2,1)} %param.25) | copy-start | bytes 16
  115.0 77.1 %copy-start.212 = (bf16[8]{0:T(256)(128)(2,1)S(1)}, bf16[8]{0:T(256)(128)(2,1)}, u32[]{:S(2)}) copy-start(bf16[8]{0:T(256)(128)(2,1)} %param.24) | copy-start | bytes 52
  115.7 266.6 %copy-start.141 = (f32[8,128]{1,0:T(8,128)}, f32[8,128]{1,0:T(8,128)S(1)}, u32[]{:S(2)}) copy-start(f32[8,128]{1,0:T(8,128)S(1)} %get-tuple-element.264) | copy-start | bytes 12292
  115.7 421.2 %copy-start.119 = (f32[8,128]{1,0:T(8,128)}, f32[8,128]{1,0:T(8,128)S(1)}, u32[]{:S(2)}) copy-start(f32[8,128]{1,0:T(8,128)S(1)} %get-tuple-element.265) | copy-start | bytes 12292
  160.1 13.8 %all-to-all-start.5 = ((bf16[64,16,256]{2,1,0:T(8,128)(2,1)}), bf16[64,16,256]{2,1,0:T(8,128)(2,1)S(1)}, u32[]{:S(2)}, u32[]{:S(2)}) async-start(bf16[64,16,256]{2,1,0:T(8,128)(2,1)} %get-tuple-element.137), calls=%async_computation.5 | async-start | bytes 1048576 | tf_op jit(solution)/shard_map/all_to_all | solution.py:238
  163.6 98.5 %copy-start.180 = (bf16[8,256]{1,0:T(8,128)(2,1)S(1)}, bf16[8,256]{1,0:T(8,128)(2,1)}, u32[]{:S(2)}) copy-start(bf16[8,256]{1,0:T(8,128)(2,1)} %param.22) | copy-start | bytes 12292
  164.1 155.3 %copy-start.144 = (f32[8,128]{1,0:T(8,128)}, f32[8,128]{1,0:T(8,128)S(1)}, u32[]{:S(2)}) copy-start(f32[8,128]{1,0:T(8,128)S(1)} %fusion.118) | copy-start | bytes 12292
  173.9 13.8 %all-to-all-start.4 = ((bf16[64,16,256]{2,1,0:T(8,128)(2,1)}), bf16[64,16,256]{2,1,0:T(8,128)(2,1)S(1)}, u32[]{:S(2)}, u32[]{:S(2)}) async-start(bf16[64,16,256]{2,1,0:T(8,128)(2,1)} %get-tuple-element.138), calls=%async_computation.4 | async-start | bytes 1048576 | tf_op jit(solution)/shard_map/all_to_all | solution.py:238
  177.5 407.4 %copy-start.127 = (f32[8,128]{1,0:T(8,128)}, f32[8,128]{1,0:T(8,128)S(1)}, u32[]{:S(2)}) copy-start(f32[8,128]{1,0:T(8,128)S(1)} %broadcast_multiply_fusion.7) | copy-start | bytes 12292
  177.5 298.0 %copy-start.129 = (f32[8,128]{1,0:T(8,128)}, f32[8,128]{1,0:T(8,128)S(1)}, u32[]{:S(2)}) copy-start(f32[8,128]{1,0:T(8,128)S(1)} %broadcast_multiply_fusion.3) | copy-start | bytes 12292
  187.6 70.2 %all-to-all-start.7 = ((bf16[64,16,256]{2,1,0:T(8,128)(2,1)}), bf16[64,16,256]{2,1,0:T(8,128)(2,1)}, u32[]{:S(2)}, u32[]{:S(2)}) async-start(bf16[64,16,256]{2,1,0:T(8,128)(2,1)} %get-tuple-element.139), calls=%async_computation.7 | async-start | bytes 1048576 | tf_op jit(solution)/shard_map/all_to_all | solution.py:238
  257.8 81.1 %copy-start.188 = (f32[1024]{0:T(1024)}, f32[1024]{0:T(1024)S(1)}, u32[]{:S(2)}) copy-start(f32[1024]{0:T(1024)S(1)} %convert_element_type.472) | copy-start | bytes 12292
  257.8 110.0 %copy-start.152 = (f32[8,128]{1,0:T(8,128)}, f32[8,128]{1,0:T(8,128)S(1)}, u32[]{:S(2)}) copy-start(f32[8,128]{1,0:T(8,128)S(1)} %fusion.196) | copy-start | bytes 12292
  257.8 124.5 %copy-start.200 = (f32[1,256]{1,0:T(1,128)}, f32[1,256]{1,0:T(1,128)S(1)}, u32[]{:S(2)}) copy-start(f32[1,256]{1,0:T(1,128)S(1)} %get-tuple-element.266) | copy-start | bytes 3076
  257.8 157.1 %copy-start.174 = (f32[1,256]{1,0:T(1,128)}, f32[1,256]{1,0:T(1,128)S(1)}, u32[]{:S(2)}) copy-start(f32[1,256]{1,0:T(1,128)S(1)} %get-tuple-element.189) | copy-start | bytes 3076
  257.8 64.3 %all-to-all-start.6 = ((bf16[64,16,256]{2,1,0:T(8,128)(2,1)}), bf16[64,16,256]{2,1,0:T(8,128)(2,1)}, u32[]{:S(2)}, u32[]{:S(2)}) async-start(bf16[64,16,256]{2,1,0:T(8,128)(2,1)} %get-tuple-element.140), calls=%async_computation.6 | async-start | bytes 1048576 | tf_op jit(solution)/shard_map/all_to_all | solution.py:238
  374.2 40.7 %copy-start.164 = (f32[8,128]{1,0:T(8,128)}, f32[8,128]{1,0:T(8,128)S(1)}, u32[]{:S(2)}) copy-start(f32[8,128]{1,0:T(8,128)S(1)} %get-tuple-element.92) | copy-start | bytes 12292
  374.3 101.2 %copy-start.132 = (f32[8,128]{1,0:T(8,128)}, f32[8,128]{1,0:T(8,128)S(1)}, u32[]{:S(2)}) copy-start(f32[8,128]{1,0:T(8,128)S(1)} %fusion.198) | copy-start | bytes 12292
  395.2 14.9 %copy-start.8 = (f32[8,128,256]{2,1,0:T(8,128)}, f32[8,128,256]{2,1,0:T(8,128)S(1)}, u32[]{:S(2)}) copy-start(f32[8,128,256]{2,1,0:T(8,128)S(1)} %get-tuple-element.238) | copy-start | bytes 3145732
  517.2 12.8 %copy-start.182 = (f32[256]{0:T(256)S(1)}, f32[256]{0:T(256)}, u32[]{:S(2)}) copy-start(f32[256]{0:T(256)} %get-tuple-element.119) | copy-start | bytes 3076
  517.2 12.9 %copy-start.179 = (f32[768]{0:T(1024)S(1)}, f32[768]{0:T(1024)}, u32[]{:S(2)}) copy-start(f32[768]{0:T(1024)} %convert_reduce_fusion.5) | copy-start | bytes 9220
  522.1 14.8 %copy-start.150 = (f32[8,128]{1,0:T(8,128)}, f32[8,128]{1,0:T(8,128)S(1)}, u32[]{:S(2)}) copy-start(f32[8,128]{1,0:T(8,128)S(1)} %multiply_multiply_fusion.12) | copy-start | bytes 12292
  523.1 29.7 %all-to-all-start.16 = ((f32[4,1,256]{2,1,0:T(1,128)}), f32[4,1,256]{2,1,0:T(1,128)S(1)}, u32[]{:S(2)}, u32[]{:S(2)}) async-start(f32[4,1,256]{2,1,0:T(1,128)} %reshape.1071), calls=%async_computation.16 | async-start | bytes 8192 | tf_op jit(solution)/shard_map/all_to_all | solution.py:33
  552.7 13.4 %all-to-all-start.14 = ((f32[4,1,256]{2,1,0:T(1,128)}), f32[4,1,256]{2,1,0:T(1,128)S(1)}, u32[]{:S(2)}, u32[]{:S(2)}) async-start(f32[4,1,256]{2,1,0:T(1,128)} %reshape.1069), calls=%async_computation.14 | async-start | bytes 8192 | tf_op jit(solution)/shard_map/all_to_all | solution.py:33
  566.2 14.5 %all-to-all-start = ((bf16[8,128,256]{2,0,1:T(8,128)(2,1)}), bf16[8,128,256]{2,0,1:T(8,128)(2,1)}, u32[]{:S(2)}, u32[]{:S(2)}) async-start(bf16[8,128,256]{2,0,1:T(8,128)(2,1)} %copy.756), calls=%async_computation | async-start | bytes 1048576 | tf_op jit(solution)/shard_map/all_to_all | solution.py:210
  572.6 12.3 %copy-start.204 = (f32[1,256]{1,0:T(1,128)S(1)}, f32[1,256]{1,0:T(1,128)}, u32[]{:S(2)}) copy-start(f32[1,256]{1,0:T(1,128)} %copy-done.200) | copy-start | bytes 3076
  580.7 14.5 %all-to-all-start.1 = ((bf16[8,128,256]{2,0,1:T(8,128)(2,1)}), bf16[8,128,256]{2,0,1:T(8,128)(2,1)}, u32[]{:S(2)}, u32[]{:S(2)}) async-start(bf16[8,128,256]{2,0,1:T(8,128)(2,1)} %copy.764), calls=%async_computation.1 | async-start | bytes 1048576 | tf_op jit(solution)/shard_map/all_to_all | solution.py:210
  595.2 14.7 %all-to-all-start.2 = ((bf16[8,128,256]{2,0,1:T(8,128)(2,1)}), bf16[8,128,256]{2,0,1:T(8,128)(2,1)}, u32[]{:S(2)}, u32[]{:S(2)}) async-start(bf16[8,128,256]{2,0,1:T(8,128)(2,1)} %copy.771), calls=%async_computation.2 | async-start | bytes 1048576 | tf_op jit(solution)/shard_map/all_to_all | solution.py:210
  609.9 14.5 %all-to-all-start.3 = ((bf16[8,128,256]{2,0,1:T(8,128)(2,1)}), bf16[8,128,256]{2,0,1:T(8,128)(2,1)}, u32[]{:S(2)}, u32[]{:S(2)}) async-start(bf16[8,128,256]{2,0,1:T(8,128)(2,1)} %copy.778), calls=%async_computation.3 | async-start | bytes 1048576 | tf_op jit(solution)/shard_map/all_to_all | solution.py:210
  618.9 11.2 %copy-start.101 = (pred[64,16]{1,0:T(8,128)(4,1)S(1)}, pred[64,16]{1,0:T(8,128)(4,1)}, u32[]{:S(2)}) copy-start(pred[64,16]{1,0:T(8,128)(4,1)} %copy-done.100) | copy-start | bytes 3076
  618.9 11.2 %copy-start.103 = (pred[64,16]{1,0:T(8,128)(4,1)S(1)}, pred[64,16]{1,0:T(8,128)(4,1)}, u32[]{:S(2)}) copy-start(pred[64,16]{1,0:T(8,128)(4,1)} %copy-done.102) | copy-start | bytes 3076
  618.9 11.2 %copy-start.105 = (pred[64,16]{1,0:T(8,128)(4,1)S(1)}, pred[64,16]{1,0:T(8,128)(4,1)}, u32[]{:S(2)}) copy-start(pred[64,16]{1,0:T(8,128)(4,1)} %copy-done.104) | copy-start | bytes 3076
  618.9 11.2 %copy-start.107 = (pred[64,16]{1,0:T(8,128)(4,1)S(1)}, pred[64,16]{1,0:T(8,128)(4,1)}, u32[]{:S(2)}) copy-start(pred[64,16]{1,0:T(8,128)(4,1)} %copy-done.106) | copy-start | bytes 3076
  618.9 11.2 %copy-start.108 = (f32[16,256]{1,0:T(8,128)S(1)}, f32[16,256]{1,0:T(8,128)}, u32[]{:S(2)}) copy-start(f32[16,256]{1,0:T(8,128)} %constant_dynamic-slice_fusion.6) | copy-start | bytes 49156
  624.4 14.8 %all-to-all-start.19 = ((f32[32,1,2]{2,1,0:T(1,128)}), f32[32,1,2]{2,1,0:T(1,128)S(1)}, u32[]{:S(2)}, u32[]{:S(2)}) async-start(f32[32,1,2]{2,1,0:T(1,128)} %bitcast.190), calls=%async_computation.19 | async-start | bytes 32768 | tf_op jit(solution)/shard_map/all_to_all | solution.py:40
  639.2 18.3 %copy-start.109 = (f32[32,1,2]{2,1,0:T(1,128)}, f32[32,1,2]{2,1,0:T(1,128)S(1)}, u32[]{:S(2)}) copy-start(f32[32,1,2]{2,1,0:T(1,128)S(1)} %all-to-all-done.19) | copy-start | bytes 772
  639.2 10.1 %all-to-all-start.8 = ((f32[4,1,256]{2,1,0:T(1,128)}), f32[4,1,256]{2,1,0:T(1,128)S(1)}, u32[]{:S(2)}, u32[]{:S(2)}) async-start(f32[4,1,256]{2,1,0:T(1,128)} %reshape.1067), calls=%async_computation.8 | async-start | bytes 8192 | tf_op jit(solution)/shard_map/all_to_all | solution.py:33
  649.3 14.6 %all-to-all-start.17 = ((f32[32,1,8]{2,1,0:T(1,128)}), f32[32,1,8]{2,1,0:T(1,128)}, u32[]{:S(2)}, u32[]{:S(2)}) async-start(f32[32,1,8]{2,1,0:T(1,128)} %copy.875), calls=%async_computation.17 | async-start | bytes 32768 | tf_op jit(solution)/shard_map/all_to_all | solution.py:40
  663.9 8.9 %all-to-all-start.20 = ((f32[4,1,4096]{2,1,0:T(1,128)}), f32[4,1,4096]{2,1,0:T(1,128)S(1)}, u32[]{:S(2)}, u32[]{:S(2)}) async-start(f32[4,1,4096]{2,1,0:T(1,128)} %reshape.1073), calls=%async_computation.20 | async-start | bytes 131072 | tf_op jit(solution)/shard_map/all_to_all | solution.py:33
  672.8 13.1 %all-to-all-start.15 = ((f32[32,4,2]{1,2,0:T(2,128)}), f32[32,4,2]{1,2,0:T(2,128)}, u32[]{:S(2)}, u32[]{:S(2)}) async-start(f32[32,4,2]{1,2,0:T(2,128)} %copy.873), calls=%async_computation.15 | async-start | bytes 65536 | tf_op jit(solution)/shard_map/all_to_all | solution.py:40
  685.9 11.8 %all-to-all-start.9 = ((f32[32,4,2]{1,2,0:T(2,128)}), f32[32,4,2]{1,2,0:T(2,128)}, u32[]{:S(2)}, u32[]{:S(2)}) async-start(f32[32,4,2]{1,2,0:T(2,128)} %copy.830), calls=%async_computation.9 | async-start | bytes 65536 | tf_op jit(solution)/shard_map/all_to_all | solution.py:40
  697.6 11.1 %all-to-all-start.21 = ((f32[32,1,128]{2,1,0:T(1,128)}), f32[32,1,128]{2,1,0:T(1,128)S(1)}, u32[]{:S(2)}, u32[]{:S(2)}) async-start(f32[32,1,128]{2,1,0:T(1,128)} %reshape.1075), calls=%async_computation.21 | async-start | bytes 32768 | tf_op jit(solution)/shard_map/all_to_all | solution.py:40
  708.7 19.7 %all-to-all-start.12 = ((f32[4,32,8,256]{3,2,1,0:T(8,128)}), f32[4,32,8,256]{3,2,1,0:T(8,128)}, u32[]{:S(2)}, u32[]{:S(2)}) async-start(f32[4,32,8,256]{3,2,1,0:T(8,128)} %bitcast.690), calls=%async_computation.12 | async-start | bytes 2097152 | tf_op jit(solution)/shard_map/all_to_all | solution.py:33
  728.6 31.1 %all-to-all-start.10 = ((f32[4,32,2,2048]{3,2,1,0:T(2,128)}), f32[4,32,2,2048]{3,2,1,0:T(2,128)}, u32[]{:S(2)}, u32[]{:S(2)}) async-start(f32[4,32,2,2048]{3,2,1,0:T(2,128)} %bitcast.649), calls=%async_computation.10 | async-start | bytes 4194304 | tf_op jit(solution)/shard_map/all_to_all | solution.py:33
  734.0 30.9 %copy-start.114 = (f32[8,128]{1,0:T(8,128)S(1)}, f32[8,128]{1,0:T(8,128)}, u32[]{:S(2)}) copy-start(f32[8,128]{1,0:T(8,128)} %copy-done.113) | copy-start | bytes 12292
  734.0 30.9 %copy-start.116 = (f32[8,128]{1,0:T(8,128)S(1)}, f32[8,128]{1,0:T(8,128)}, u32[]{:S(2)}) copy-start(f32[8,128]{1,0:T(8,128)} %copy-done.115) | copy-start | bytes 12292
  734.0 30.9 %copy-start.122 = (f32[8,128]{1,0:T(8,128)S(1)}, f32[8,128]{1,0:T(8,128)}, u32[]{:S(2)}) copy-start(f32[8,128]{1,0:T(8,128)} %copy-done.121) | copy-start | bytes 12292
  734.0 30.9 %copy-start.124 = (f32[8,128]{1,0:T(8,128)S(1)}, f32[8,128]{1,0:T(8,128)}, u32[]{:S(2)}) copy-start(f32[8,128]{1,0:T(8,128)} %copy-done.123) | copy-start | bytes 12292
  734.0 30.9 %copy-start.128 = (f32[8,128]{1,0:T(8,128)S(1)}, f32[8,128]{1,0:T(8,128)}, u32[]{:S(2)}) copy-start(f32[8,128]{1,0:T(8,128)} %copy-done.127) | copy-start | bytes 12292
  734.0 30.9 %copy-start.131 = (f32[8,128]{1,0:T(8,128)S(1)}, f32[8,128]{1,0:T(8,128)}, u32[]{:S(2)}) copy-start(f32[8,128]{1,0:T(8,128)} %copy-done.129) | copy-start | bytes 12292
  734.0 30.9 %copy-start.134 = (f32[8,128]{1,0:T(8,128)S(1)}, f32[8,128]{1,0:T(8,128)}, u32[]{:S(2)}) copy-start(f32[8,128]{1,0:T(8,128)} %copy-done.132) | copy-start | bytes 12292
  734.0 30.9 %copy-start.140 = (f32[8,128]{1,0:T(8,128)S(1)}, f32[8,128]{1,0:T(8,128)}, u32[]{:S(2)}) copy-start(f32[8,128]{1,0:T(8,128)} %copy-done.138) | copy-start | bytes 12292
  739.0 26.0 %copy-start.21 = (f32[8,128,256]{2,1,0:T(8,128)S(1)}, f32[8,128,256]{2,1,0:T(8,128)}, u32[]{:S(2)}) copy-start(f32[8,128,256]{2,1,0:T(8,128)} %copy-done.20) | copy-start | bytes 3145732
  759.6 16.4 %all-to-all-start.13 = ((f32[32,8,256]{2,1,0:T(8,128)}), f32[32,8,256]{2,1,0:T(8,128)S(1)}, u32[]{:S(2)}, u32[]{:S(2)}) async-start(f32[32,8,256]{2,1,0:T(8,128)} %reduce_sum.1062), calls=%async_computation.13 | async-start | bytes 524288 | tf_op jit(solution)/shard_map/all_to_all | solution.py:40
  771.3 16.3 %copy-start.90 = (bf16[1,1,64,16,256]{4,3,2,1,0:T(8,128)(2,1)S(1)}, bf16[1,1,64,16,256]{4,3,2,1,0:T(8,128)(2,1)}, u32[]{:S(2)}) copy-start(bf16[1,1,64,16,256]{4,3,2,1,0:T(8,128)(2,1)} %get-tuple-element.157) | copy-start | bytes 1572868
  771.3 16.3 %copy-start.91 = (bf16[1,1,64,16,256]{4,3,2,1,0:T(8,128)(2,1)S(1)}, bf16[1,1,64,16,256]{4,3,2,1,0:T(8,128)(2,1)}, u32[]{:S(2)}) copy-start(bf16[1,1,64,16,256]{4,3,2,1,0:T(8,128)(2,1)} %get-tuple-element.158) | copy-start | bytes 1572868
  771.3 16.3 %copy-start.92 = (bf16[1,1,64,16,256]{4,3,2,1,0:T(8,128)(2,1)S(1)}, bf16[1,1,64,16,256]{4,3,2,1,0:T(8,128)(2,1)}, u32[]{:S(2)}) copy-start(bf16[1,1,64,16,256]{4,3,2,1,0:T(8,128)(2,1)} %get-tuple-element.159) | copy-start | bytes 1572868
  771.3 16.3 %copy-start.93 = (bf16[1,1,64,16,256]{4,3,2,1,0:T(8,128)(2,1)S(1)}, bf16[1,1,64,16,256]{4,3,2,1,0:T(8,128)(2,1)}, u32[]{:S(2)}) copy-start(bf16[1,1,64,16,256]{4,3,2,1,0:T(8,128)(2,1)} %get-tuple-element.164) | copy-start | bytes 1572868
  776.1 19.3 %all-to-all-start.11 = ((f32[32,2,2048]{2,1,0:T(2,128)}), f32[32,2,2048]{2,1,0:T(2,128)S(1)}, u32[]{:S(2)}, u32[]{:S(2)}) async-start(f32[32,2,2048]{2,1,0:T(2,128)} %reduce_sum.1060), calls=%async_computation.11 | async-start | bytes 1048576 | tf_op jit(solution)/shard_map/all_to_all | solution.py:40
  (177 other events, 612.5 us)
Sparse Core Ops, SparseCore 0:
  11.4 66.0 all-gather.5
where the time goes:
time: 815 us; the launch traced here: 804 us
  blocking collectives  257 us (32%)
  matrix products  137 us (17%)
  local copies, waits for them, and re-layouts  131 us (16%)
  starting transfers between devices  100 us (12%)
  waiting for transfers between devices  83.9 us (10%)
  other arithmetic  79.6 us (10%)
  between operations  17.1 us (2%)
    unnamed x1, blocking collectives  64.9 us
    all_gather x1, blocking collectives, fetch_weights(): lax.all_gather(w_down, SEQ_DP, axis=0, tiled=True)  55.7 us
    all_gather x1, blocking collectives, fetch_weights(): lax.all_gather(proj_biases, SEQ_DP, axis=1, tiled=True)  48.9 us
    all_gather x1, blocking collectives, sent_together(): lax.all_gather(both, axis, axis=dim, tiled=True)  44.2 us
    all_gather x1, blocking collectives, fetch_weights(): lax.all_gather(time_embed, SEQ_DP, axis=1, tiled=True)  42.8 us
    all_to_all x7, starting transfers between devices, summed_rows(): return jnp.sum(lax.all_to_all(own, far, 0, 0, tiled=True), axis=0)  38.4 us
    all_to_all x7, starting transfers between devices, summed_on_arrival(): lax.all_to_all(parts, axis, split_axis=0, concat_axis=0, tiled=True)  29.5 us
    unnamed x456, local copies, waits for them, and re-layouts  25.5 us
  transfers between devices with their start and end apart: 23, of which 15 were waited for; matrix products, arithmetic and copies ran while one was open for 19% of the time, Pallas kernels for 0%

commit v1 on v0

v1 whole, which is shorter than its diff:
```python
import functools

import jax
import jax.numpy as jnp
from jax import lax
from jax.experimental import pallas as pl
from jax.experimental.pallas import tpu as pltpu
from jax.sharding import PartitionSpec as P

f32, bf16, i32 = jnp.float32, jnp.bfloat16, jnp.int32
EPS = 1e-5
BIG = 1e30
D, FF, SL, MICRO, TRAJ = 256, 1024, 128, 4, 64
NT = 32
PART = 512
GELU_A = 0.7978845608028654
GELU_B = 0.044715
CAPS = (304, 240, 192, 160, 128, 80, 64, 48)
FULL = (PART,) * 8
MESH = pl.DeviceIdType.MESH
VMEM_LIMIT = 56 * 2**20

TE, GAIN, SHIFT, BIAS, MASK, UP, FLAG = 0, 64, 66, 68, 72, 80, 96


def nt_dot(a, b):
    return lax.dot_general(a, b, (((1,), (1,)), ((), ())), preferred_element_type=f32)


def nn_dot(a, b):
    return lax.dot_general(a, b, (((1,), (0,)), ((), ())), preferred_element_type=f32)


def tn_dot(a, b):
    return lax.dot_general(a, b, (((0,), (0,)), ((), ())), preferred_element_type=f32)


def iota(shape, dim):
    return lax.broadcasted_iota(i32, shape, dim)


def one_zero(cond):
    return jnp.where(cond, 1.0, 0.0)


def fold8(v):
    n = v.shape[0] // 8
    return jnp.sum(v.reshape(n, 8, v.shape[1]), axis=0)


def bases(caps):
    out, at = [], 0
    for c in caps:
        out.append(at)
        at += c
    return out


def decode_room(caps):
    most = max(caps)
    return most, -(-(most + 16) // SL) * SL


class Place:
    def __init__(self):
        self.seq = lax.axis_index("seq")
        self.dp = lax.axis_index("dp")
        self.x, self.core = self.seq // 2, self.seq % 2
        self.z, self.y = self.dp // 4, self.dp % 4

    def seq_peer(self, k):
        return ((self.seq + k) % 8, self.dp)

    def x_peer(self, k):
        return ((self.seq + 2 * k) % 8, self.dp)

    def y_peer(self, k):
        return (self.seq, self.z * 4 + (self.y + k) % 4)

    def z_peer(self, k):
        return (self.seq, ((self.z + k) % 4) * 4 + self.y)

    def sibling(self):
        return (self.seq + 1 - 2 * self.core, self.dp)

    def greet(self, everyone=True):
        peers = [self.seq_peer(k) for k in range(1, 8)]
        if everyone:
            peers += [self.y_peer(k) for k in range(1, 4)] + [self.z_peer(k) for k in range(1, 4)]
        barrier = pltpu.get_barrier_semaphore()
        for peer in peers:
            pl.semaphore_signal(barrier, inc=1, device_id=peer, device_id_type=MESH)
        return barrier, len(peers)


def remote(src, dst, send_sem, recv_sem, peer):
    return pltpu.make_async_remote_copy(
        src_ref=src, dst_ref=dst, send_sem=send_sem, recv_sem=recv_sem, device_id=peer, device_id_type=MESH
    )


def mask_rows(len_ref, vis_ref):
    eye = one_zero(iota((TRAJ, TRAJ), 0) == iota((TRAJ, TRAJ), 1)).astype(bf16)
    step = (iota((TRAJ, SL), 1) // 2).astype(f32)
    valid, shown = [], []
    for m in range(MICRO):
        row = jnp.broadcast_to(len_ref[m : m + 1, :].astype(f32), (SL, TRAJ)).astype(bf16)
        valid.append(one_zero(step < nt_dot(eye, row)))
        shown.append(one_zero(vis_ref[m] > 0))
    return jnp.concatenate(valid, axis=0), jnp.concatenate(shown, axis=0)


def part_lanes(valid, shown, part):
    n = MICRO * TRAJ
    pick = one_zero(iota((SL, PART), 0) == 16 * part + iota((SL, PART), 1) % 16).astype(bf16)
    row, lane = iota((n, PART), 0), iota((n, PART), 1)
    mine = (row // TRAJ == lane // SL) & (row % 8 == (lane % SL) // 16)
    group = one_zero((iota((16, n), 1) % TRAJ) // 8 == iota((16, n), 0)).astype(bf16)

    def lanes(mask):
        spread = nn_dot(mask.astype(bf16), pick)
        return nn_dot(group, jnp.where(mine, spread, 0.0).astype(bf16))[:8]

    return lanes(valid), lanes(shown)


def part_ranks(open_lanes):
    r, c = iota((PART, PART), 0), iota((PART, PART), 1)
    tri = (one_zero(r < c) - jnp.where(r == c, 512.0, 0.0)).astype(bf16)
    rows = jnp.concatenate([open_lanes, jnp.zeros((8, PART), f32)], axis=0).astype(bf16)
    return nn_dot(rows, tri)[:8]


def pack_part(caps, owner, rank_ref, ext_ref, dg_ref):
    most = max(caps)
    row = iota((most, PART), 0).astype(f32)
    hit = one_zero(rank_ref[pl.ds(owner, 1), :] + 512.0 == row)
    lhs = jnp.concatenate([hit, ext_ref[owner]], axis=0).astype(bf16)
    first = pl.multiple_of(owner * 8, 8)
    parts = [dg_ref[m, pl.ds(first, 8)].reshape(SL, D) for m in range(MICRO)]
    return nn_dot(lhs, jnp.concatenate(parts, axis=0))


def prepare_part(me, len_ref, vis_ref, rank_scr, ext_scr):
    valid, shown = mask_rows(len_ref, vis_ref)
    v8, s8 = part_lanes(valid, shown, me.seq)
    rank_scr[...] = part_ranks(v8 * s8)
    lane_step = (iota((8, PART), 1) % 16) // 2
    step_row = iota((8, PART), 0)
    for i in range(8):
        v = v8[i : i + 1, :]
        steps = jnp.where(lane_step == step_row, jnp.broadcast_to(v, (8, PART)), 0.0)
        hidden = jnp.where(step_row == 0, jnp.broadcast_to(v * (1.0 - s8[i : i + 1, :]), (8, PART)), 0.0)
        ext_scr[i] = jnp.concatenate([steps, hidden], axis=0)
    return valid, shown


def send_part(caps, me, k, dg_ref, rank_scr, ext_scr, buf, r_ref, sends, recvs):
    most = max(caps)
    base = bases(caps)
    owner = (me.seq + k) % 8
    got = pack_part(caps, owner, rank_scr, ext_scr, dg_ref)
    buf[k] = got[:most].astype(bf16)
    for j in range(8):
        @pl.when(me.seq == j)
        def _():
            there = r_ref.at[pl.ds(base[j], caps[j])]
            if k == 0:
                there[...] = buf[k, : caps[j]]
            else:
                remote(buf.at[k, pl.ds(0, caps[j])], there, sends.at[k], recvs.at[j], me.seq_peer(k)).start()
    return got[most:]


def finish_parts(caps, me, buf, r_ref, sends, recvs):
    base = bases(caps)
    for j in range(8):
        @pl.when(me.seq != j)
        def _():
            here = r_ref.at[pl.ds(base[j], caps[j])]
            pltpu.make_async_copy(here, here, recvs.at[j]).wait()

        @pl.when(me.seq == j)
        def _():
            for k in range(1, 8):
                there = buf.at[k, pl.ds(0, caps[j])]
                pltpu.make_async_copy(there, there, sends.at[k]).wait()


def exchange_kernel(caps, len_ref, vis_ref, dg_ref, r_ref, rank_scr, ext_scr, buf, sends, recvs):
    me = Place()
    barrier, count = me.greet(everyone=False)
    prepare_part(me, len_ref, vis_ref, rank_scr, ext_scr)
    pl.semaphore_wait(barrier, count)
    for k in range(8):
        send_part(caps, me, k, dg_ref, rank_scr, ext_scr, buf, r_ref, sends, recvs)
    finish_parts(caps, me, buf, r_ref, sends, recvs)


def vmem():
    return pl.BlockSpec(memory_space=pltpu.VMEM)


def part_scratch(caps):
    return [
        pltpu.VMEM((8, PART), f32),
        pltpu.VMEM((8, 16, PART), f32),
        pltpu.VMEM((8, max(caps), D), bf16),
        pltpu.SemaphoreType.DMA((8,)),
        pltpu.SemaphoreType.DMA((8,)),
    ]


def exchange(caps, lengths, visible, dec_grad, cid):
    return pl.pallas_call(
        functools.partial(exchange_kernel, caps),
        out_shape=jax.ShapeDtypeStruct((sum(caps), D), bf16),
        in_specs=[vmem()] * 3,
        out_specs=vmem(),
        scratch_shapes=part_scratch(caps),
        compiler_params=pltpu.CompilerParams(collective_id=cid, has_side_effects=True, vmem_limit_bytes=VMEM_LIMIT),
        name="exchange_gradients",
    )(lengths, visible, dec_grad)


def gather_kernel(
    caps, len_ref, vis_ref, dg_ref, wq_ref, wo_ref, wu_ref, wd_ref, small_ref,
    w_out, wdn_out, sm_out, r_ref, open_out, count_out, part_out,
    rank_scr, ext_scr, buf, sends, recvs, slabs, open_scr, s1, r1, s2a, r2a, s2b, r2b, s3, r3,
):
    me = Place()
    barrier, count = me.greet()
    half, x2 = me.x // 2, me.x % 2
    own = (me.z + half * (me.y - me.z), me.y + half * (me.z - me.y))

    valid, shown = mask_rows(len_ref, vis_ref)
    opened = valid * shown
    open_scr[...] = opened
    n = MICRO * TRAJ
    group = one_zero((iota((16, n), 1) % TRAJ) // 8 == iota((16, n), 0)).astype(bf16)
    blk = one_zero(iota((SL, SL), 0) // 16 == iota((SL, SL), 1) // 16).astype(bf16)
    pairs = nn_dot(nn_dot(group, opened.astype(bf16)).astype(bf16), blk)
    lane_blk = iota((16, SL), 1) // 16
    room = jnp.zeros((16, SL), f32)
    for j in range(8):
        room = jnp.where(lane_blk == j, float(caps[j]), room)
    over = jnp.max(jnp.max(one_zero(pairs > room), axis=1, keepdims=True), axis=0, keepdims=True)

    small = small_ref[...].astype(f32)
    small = jnp.where(iota((2, SL), 1) == FLAG, jnp.broadcast_to(over, (2, SL)), small)
    small = jnp.concatenate([small, jnp.zeros((2, SL), f32)], axis=1)
    rows = []
    for f in range(2):
        one = slice(f, f + 1)
        rows += [wq_ref[one, c : c + D].astype(f32) for c in range(0, 3 * D, D)]
        rows += [wo_ref[one, :].astype(f32)]
        rows += [wu_ref[one, c : c + D].astype(f32) for c in range(0, 4 * D, D)]
        rows += [small[one]]
    slab = jnp.concatenate(rows + [wd_ref[...].astype(f32), jnp.zeros((6, D), f32)], axis=0)
    mine = slabs.at[half, me.core, own[0], own[1], x2]
    mine[...] = slab.astype(bf16)

    pl.semaphore_wait(barrier, count)
    step1 = [remote(mine, mine, s1.at[k], r1.at[k], me.x_peer(k + 1)) for k in range(3)]
    for c in step1:
        c.start()

    v8, s8 = part_lanes(valid, shown, me.seq)
    rank_scr[...] = part_ranks(v8 * s8)
    lane_step = (iota((8, PART), 1) % 16) // 2
    step_row = iota((8, PART), 0)
    for i in range(8):
        v = v8[i : i + 1, :]
        steps = jnp.where(lane_step == step_row, jnp.broadcast_to(v, (8, PART)), 0.0)
        hidden = jnp.where(step_row == 0, jnp.broadcast_to(v * (1.0 - s8[i : i + 1, :]), (8, PART)), 0.0)
        ext_scr[i] = jnp.concatenate([steps, hidden], axis=0)

    def send(k):
        return send_part(caps, me, k, dg_ref, rank_scr, ext_scr, buf, r_ref, sends, recvs)

    sums = jnp.zeros((16, D), f32)
    for k in (4, 3, 5, 2):
        sums = sums + send(k)
    for c in step1:
        c.wait()
    step2a = []
    row_a = slabs.at[0, me.core, me.z, me.y]
    row_b = slabs.at[1, me.core, me.y, me.z]
    for k in range(3):
        step2a.append(remote(row_a, row_a, s2a.at[0, k], r2a.at[0, k], me.y_peer(k + 1)))
        step2a.append(remote(row_b, row_b, s2a.at[1, k], r2a.at[1, k], me.z_peer(k + 1)))
    for c in step2a:
        c.start()
    for k in (6, 1, 7, 0):
        sums = sums + send(k)
    for c in step2a:
        c.wait()
    all_a = slabs.at[0, me.core, me.z]
    all_b = slabs.at[1, me.core, me.y]
    step2b, step3 = [], []
    for k in range(3):
        step2b.append(remote(all_a, all_a, s2b.at[0, k], r2b.at[0, k], me.z_peer(k + 1)))
        step2b.append(remote(all_b, all_b, s2b.at[1, k], r2b.at[1, k], me.y_peer(k + 1)))
    for c in step2b:
        c.start()
    step3.append(remote(all_a, all_a, s3.at[0, 0], r3.at[0, 0], me.sibling()))
    step3.append(remote(all_b, all_b, s3.at[1, 0], r3.at[1, 0], me.sibling()))
    for c in step3:
        c.start()

    for m in range(MICRO):
        open_out[8 * m : 8 * m + 8, :] = open_scr[pl.ds(pl.multiple_of(m * TRAJ + 8 * me.seq, 8), 8), :]
    counted = jnp.concatenate([open_out[...], jnp.zeros((SL - NT, SL), f32)], axis=0).astype(bf16)
    count_out[...] = nt_dot(jnp.ones((16, SL), bf16), counted)[:8].astype(i32)
    part_out[...] = jnp.zeros_like(part_out)
    part_out[pl.ds(pl.multiple_of(8 * me.seq, 8), 8), :] = sums[:8]
    part_out[MASK : MASK + 1, :] = sums[8:9]

    for k in range(3):
        for h in range(2):
            step2b[2 * k + h].wait()
            from_row = ((me.z if h == 0 else me.y) + 3 - k) % 4
            part = slabs.at[h, me.core, from_row]
            c = remote(part, part, s3.at[h, k + 1], r3.at[h, k + 1], me.sibling())
            c.start()
            step3.append(c)
    for c in step3:
        c.wait()

    pr, pc = iota((D, D), 0), iota((D, D), 1)
    want = jnp.where(
        pr < 144,
        ((pr % 16) // 2) * 32 + (pr % 2) * 9 + pr // 16,
        jnp.where(pr < 208, ((pr - 144) // 8) * 32 + 18 + (pr - 144) % 8, -1),
    )
    perm = one_zero(want == pc).astype(bf16)
    feature_rows = []
    for q in range(16):
        seq, z0 = q // 2, (q % 2) * 2
        x, core = seq // 2, seq % 2
        chunk = []
        for z in (z0, z0 + 1):
            for y in range(4):
                a, b = (z, y) if x < 2 else (y, z)
                chunk.append(slabs[x // 2, core, a, b, x % 2])
        got = nn_dot(perm, jnp.concatenate(chunk, axis=0)).astype(bf16)
        for b in range(8):
            w_out[16 * q : 16 * q + 16, b * D : (b + 1) * D] = got[16 * b : 16 * b + 16]
        feature_rows.append(got[128:144, :SL])
        wdn_out[64 * q : 64 * q + 64, :] = got[144:208]
    features = jnp.concatenate(feature_rows, axis=0)
    eye = one_zero(iota((SL, SL), 0) == iota((SL, SL), 1)).astype(bf16)
    sm_out[...] = nt_dot(eye, features)
    even = one_zero(iota((SL, D), 1) == 2 * iota((SL, D), 0)).astype(bf16)
    by_device = nn_dot(even, features).astype(bf16)
    spread = one_zero(iota((SL, FF), 0) == UP + iota((SL, FF), 1) % 8).astype(bf16)
    wide = jnp.where(iota((SL, FF), 0) == iota((SL, FF), 1) // 8, nn_dot(by_device, spread), 0.0).astype(bf16)
    up = nn_dot(jnp.ones((16, SL), bf16), wide)[:1]
    for c in range(4):
        sm_out[UP + c : UP + c + 1, :] = up[:, c * D : (c + 1) * D]

    finish_parts(caps, me, buf, r_ref, sends, recvs)


def gather(caps, lengths, visible, dec_grad, w_qkv, w_out, w_up, w_down, small, cid):
    dma = pltpu.SemaphoreType.DMA
    return pl.pallas_call(
        functools.partial(gather_kernel, caps),
        out_shape=(
            jax.ShapeDtypeStruct((D, 8 * D), bf16),
            jax.ShapeDtypeStruct((FF, D), bf16),
            jax.ShapeDtypeStruct((SL, D), f32),
            jax.ShapeDtypeStruct((sum(caps), D), bf16),
            jax.ShapeDtypeStruct((NT, SL), f32),
            jax.ShapeDtypeStruct((8, SL), i32),
            jax.ShapeDtypeStruct((SL, D), f32),
        ),
        in_specs=[vmem()] * 8,
        out_specs=(vmem(),) * 7,
        scratch_shapes=part_scratch(caps) + [
            pltpu.VMEM((2, 2, 4, 4, 2, 32, D), bf16),
            pltpu.VMEM((MICRO * TRAJ, SL), f32),
            dma((3,)), dma((3,)), dma((2, 3)), dma((2, 3)), dma((2, 3)), dma((2, 3)), dma((2, 4)), dma((2, 4)),
        ],
        compiler_params=pltpu.CompilerParams(collective_id=cid, has_side_effects=True, vmem_limit_bytes=VMEM_LIMIT),
        name="gather_and_exchange",
    )(lengths, visible, dec_grad, w_qkv, w_out, w_up, w_down, small)


def encoder_kernel(caps, nt_ref, o_ref, tok_ref, w_ref, wd_ref, sm_ref, r_ref, gpart_ref,
              gtok_ref, s_ref, gs_ref,
              x_scr, src_scr, srct_scr, g_scr, gw_scr, gwd_scr, sums_scr, bup_scr, pp_scr, qkv_scr, gqkv_scr, hilo_scr,
              bin_smem, start_smem):
    rtot = sum(caps)
    lane1 = iota((1, SL), 1)
    stv = jnp.zeros((1, SL), f32)
    env = jnp.zeros((1, SL), f32)
    bnv = jnp.full((1, SL), -1.0, f32)
    b = jnp.int32(0)
    off = jnp.int32(0)
    for t in range(NT):
        n = nt_ref[0, t]
        over = (off + n) > SL
        b = jnp.where(over, b + 1, b)
        off = jnp.where(over, 0, off)
        bin_smem[t] = b
        start_smem[t] = off
        here = lane1 == t
        stv = jnp.where(here, off.astype(f32), stv)
        env = jnp.where(here, (off + n).astype(f32), env)
        bnv = jnp.where(here, b.astype(f32), bnv)
        off = off + n
    nb = b + 1
    nsup = (nb + 1) // 2

    ri = iota((SL, SL), 0)
    ci = iota((SL, SL), 1)
    o_all = o_ref[...].astype(bf16)
    tri_u = jnp.where(ri < ci, 1.0, 0.0) - jnp.where(ri == ci, 256.0, 0.0)
    pp_scr[...] = nn_dot(o_all, tri_u.astype(bf16))
    same_blk = (ri // 16) == (ci // 16)
    tri_b = jnp.where(same_blk & (ri < ci), 1.0, 0.0).astype(bf16)
    r32 = iota((NT, NT), 0)
    c32 = iota((NT, NT), 1)
    before = nn_dot(jnp.where(c32 < r32, 1.0, 0.0).astype(bf16), o_all)
    base, at = [], 0
    for c in caps:
        base.append(at)
        at += c
    lane_blk = iota((NT, SL), 1) // 16
    base_v = jnp.zeros((NT, SL), f32)
    for j in range(8):
        base_v = jnp.where(lane_blk == j, float(base[j]), base_v)
    srcv = base_v + 1.0 + nn_dot(o_all, tri_b) + nn_dot(before.astype(bf16), jnp.where(same_blk, 1.0, 0.0).astype(bf16))
    hi = jnp.floor(srcv * (1.0 / 256.0)) * 256.0
    hilo_scr[:, :SL] = hi
    hilo_scr[:, SL:] = srcv - hi

    rif = ri.astype(f32)

    def pack(t, _):
        bt = bin_smem[t]
        st = start_smem[t]
        row = pp_scr[pl.ds(t, 1), :] + (st + 256).astype(f32)
        p = jnp.where(rif == row, 1.0, 0.0).astype(bf16)
        xp = nn_dot(p, tok_ref[t])
        p2 = jnp.concatenate([p, p], axis=1)
        hl = hilo_scr[pl.ds(t, 1), :]
        sp = nt_dot(p2, jnp.broadcast_to(hl, (SL, 2 * SL)).astype(bf16))
        st8 = nt_dot(jnp.broadcast_to(hl, (16, 2 * SL)).astype(bf16), p2)[:8]

        @pl.when(st == 0)
        def _():
            x_scr[bt] = xp
            src_scr[bt] = sp
            srct_scr[bt] = st8

        @pl.when(st != 0)
        def _():
            x_scr[bt] += xp
            src_scr[bt] += sp
            srct_scr[bt] += st8

        return 0

    @pl.when(nb % 2 == 1)
    def _():
        x_scr[nb] = jnp.zeros((SL, D), f32)
        src_scr[nb] = jnp.zeros((SL, SL), f32)
        srct_scr[nb] = jnp.zeros((8, SL), f32)

    lax.fori_loop(0, NT, pack, 0)

    gw_scr[...] = jnp.zeros_like(gw_scr)
    gwd_scr[...] = jnp.zeros_like(gwd_scr)
    sums_scr[...] = jnp.zeros_like(sums_scr)
    bup_scr[...] = jnp.zeros_like(bup_scr)
    s_ref[...] = jnp.zeros_like(s_ref)

    gain1, gain2 = sm_ref[64:65, :], sm_ref[65:66, :]
    shift1, shift2 = sm_ref[66:67, :], sm_ref[67:68, :]
    bq, bv, bo, bd = (sm_ref[68 + k : 69 + k, :] for k in range(4))
    M = 2 * SL
    lane128 = iota((SL, SL), 1)
    head0 = lane128 < 64
    zero_b = jnp.zeros((SL, SL), bf16)
    ind2 = jnp.concatenate([jnp.where(head0, 1.0, 0.0), jnp.where(head0, 0.0, 1.0)], axis=0).astype(bf16)

    def two(a):
        return jnp.concatenate([jnp.where(head0, a, zero_b), jnp.where(head0, zero_b, a)], axis=0)

    def body(s, _):
        b0 = 2 * s
        x = jnp.concatenate([x_scr[b0], x_scr[b0 + 1]], axis=0)
        mean = jnp.mean(x, axis=1, keepdims=True)
        cen = x - mean
        r1 = lax.rsqrt(jnp.mean(cen * cen, axis=1, keepdims=True) + EPS)
        xh1 = cen * r1
        nf = (xh1 * gain1 + shift1).astype(bf16)
        qkv_scr[:, :D] = ((nn_dot(nf, w_ref[:, :D]) + bq).astype(bf16) * jnp.asarray(0.125, bf16))
        qkv_scr[:, D:2 * D] = nn_dot(nf, w_ref[:, D:2 * D]).astype(bf16)
        qkv_scr[:, 2 * D:3 * D] = (nn_dot(nf, w_ref[:, 2 * D:3 * D]) + bv).astype(bf16)
        saved = []
        att_rows = []
        for h in range(2):
            rows = slice(h * SL, (h + 1) * SL)
            bf_ = (b0 + h).astype(f32)
            e_seg = jnp.where((rif >= stv) & (rif < env) & (bnv == bf_), 1.0, 0.0)
            ke = ((e_seg - 1.0) * BIG).astype(bf16)
            e_seg = e_seg.astype(bf16)
            ke2 = jnp.concatenate([ke, ke], axis=0)
            cols = []
            for p in range(2):
                q = qkv_scr[rows, p * SL:(p + 1) * SL]
                k = qkv_scr[rows, D + p * SL:D + (p + 1) * SL]
                v = qkv_scr[rows, 2 * D + p * SL:2 * D + (p + 1) * SL]
                k2, v2 = two(k), two(v)
                qx = jnp.concatenate([q, e_seg], axis=1)
                kx = jnp.concatenate([k2, ke2], axis=1)
                sc = nt_dot(qx, kx)
                m0 = jnp.max(sc[:, :SL], axis=1, keepdims=True)
                m1 = jnp.max(sc[:, SL:], axis=1, keepdims=True)
                e = jnp.concatenate([jnp.exp(sc[:, :SL] - m0), jnp.exp(sc[:, SL:] - m1)], axis=1).astype(bf16)
                y = nn_dot(e, jnp.concatenate([v2, ind2], axis=1))
                rinv = 1.0 / y[:, SL:]
                att = y[:, :SL] * rinv
                cols.append(att)
                saved.append((e, rinv, att))
            att_rows.append(jnp.concatenate(cols, axis=1))
        att = jnp.concatenate(att_rows, axis=0).astype(bf16)
        mixed = x + nn_dot(att, w_ref[:, 3 * D:4 * D]) + bo
        mean = jnp.mean(mixed, axis=1, keepdims=True)
        cen = mixed - mean
        r2 = lax.rsqrt(jnp.mean(cen * cen, axis=1, keepdims=True) + EPS)
        xh2 = cen * r2
        ns = (xh2 * gain2 + shift2).astype(bf16)

        srcm = jnp.concatenate([src_scr[b0], src_scr[b0 + 1]], axis=0)
        lane_m = iota((M, SL), 1).astype(f32)
        ge = jnp.zeros((M, D), f32)
        for c0 in range(0, rtot, 256):
            cw = min(256, rtot - c0)
            oh = [jnp.where(srcm[:, :w] == lane_m[:, :w] + float(c0 + c1 + 1), 1.0, 0.0)
                  for c1 in range(0, cw, SL) for w in [min(SL, cw - c1)]]
            oh = jnp.concatenate(oh, axis=1).astype(bf16)
            ge = ge + nn_dot(oh, r_ref[c0:c0 + cw, :])
        ge_b = ge.astype(bf16)

        enc = mixed + bd
        gns = jnp.zeros((M, D), f32)
        for c in range(4):
            cs = slice(c * D, (c + 1) * D)
            ws = slice(4 * D + c * D, 5 * D + c * D)
            wup = w_ref[:, ws]
            wdn = wd_ref[cs, :]
            v = nn_dot(ns, wup) + sm_ref[UP + c : UP + c + 1, :]
            vv = v * v
            a = 0.5 * jnp.tanh(v * (vv * (GELU_A * GELU_B) + GELU_A)) + 0.5
            hact = v * a
            dg = a + hact * (1.0 - a) * (vv * (6.0 * GELU_A * GELU_B) + 2.0 * GELU_A)
            hb = hact.astype(bf16)
            enc = enc + nn_dot(hb, wdn)
            gh = (nt_dot(ge_b, wdn) * dg)
            ghb = gh.astype(bf16)
            bup_scr[:, cs] += fold8(ghb.astype(f32))
            gns = gns + nt_dot(ghb, wup)
            gw_scr[:, ws] += tn_dot(ns, ghb)
            gwd_scr[:, cs] += tn_dot(ge_b, hb)
        encb = enc.astype(bf16)
        srow = jnp.concatenate([srct_scr[b0][:1], srct_scr[b0 + 1][:1]], axis=1)
        for c0 in range(0, rtot, 256):
            cw = min(256, rtot - c0)
            oht = jnp.where(iota((cw, M), 0).astype(f32) + float(c0 + 1) == srow, 1.0, 0.0).astype(bf16)
            s_ref[c0:c0 + cw, :] += nn_dot(oht, encb).astype(bf16)

        sums_scr[7] += fold8(ge)
        sums_scr[1] += fold8(gns * xh2)
        sums_scr[3] += fold8(gns)
        eg = gns * gain2
        gmix = ge + r2 * (eg - jnp.mean(eg, axis=1, keepdims=True) - xh2 * jnp.mean(eg * xh2, axis=1, keepdims=True))
        gao = gmix.astype(bf16)
        sums_scr[6] += fold8(gao.astype(f32))
        gw_scr[:, 3 * D:4 * D] += tn_dot(att, gao)
        gatt = nt_dot(gao, w_ref[:, 3 * D:4 * D])
        for h in range(2):
            rows = slice(h * SL, (h + 1) * SL)
            bf_ = (b0 + h).astype(f32)
            e_seg = jnp.where((rif >= stv) & (rif < env) & (bnv == bf_), 1.0, 0.0)
            ke = ((e_seg - 1.0) * BIG).astype(bf16)
            e_seg = e_seg.astype(bf16)
            e_seg2 = jnp.concatenate([e_seg, e_seg], axis=0)
            for p in range(2):
                q = qkv_scr[rows, p * SL:(p + 1) * SL]
                k = qkv_scr[rows, D + p * SL:D + (p + 1) * SL]
                v = qkv_scr[rows, 2 * D + p * SL:2 * D + (p + 1) * SL]
                k2, v2, q2 = two(k), two(v), two(q)
                e, rinv, at_ = saved[2 * h + p]
                da = gatt[rows, p * SL:(p + 1) * SL] * rinv
                dao = (da * at_).astype(bf16)
                da = da.astype(bf16)
                dp = nt_dot(jnp.concatenate([da, dao], axis=1), jnp.concatenate([v2, -ind2], axis=1))
                gsc = (e.astype(f32) * dp).astype(bf16)
                gq = nn_dot(gsc, k2) * 0.125
                da2, dao2 = two(da), two(dao)
                st_ = nt_dot(jnp.concatenate([k, ke], axis=1), jnp.concatenate([q2, e_seg2], axis=1))
                et = jnp.exp(st_ - jnp.max(st_, axis=0, keepdims=True)).astype(bf16)
                dpt = nt_dot(jnp.concatenate([v, jnp.full((SL, SL), -1.0, bf16)], axis=1), jnp.concatenate([da2, dao2], axis=1))
                gst = (et.astype(f32) * dpt).astype(bf16)
                gv = nn_dot(et, da2)
                gk = nn_dot(gst, q2)
                gqkv_scr[rows, p * SL:(p + 1) * SL] = gq.astype(bf16)
                gqkv_scr[rows, D + p * SL:D + (p + 1) * SL] = gk.astype(bf16)
                gqkv_scr[rows, 2 * D + p * SL:2 * D + (p + 1) * SL] = gv.astype(bf16)
        gqkv = gqkv_scr[...]
        sums_scr[4] += fold8(gqkv[:, :D].astype(f32))
        sums_scr[5] += fold8(gqkv[:, 2 * D:].astype(f32))
        gw_scr[:, :3 * D] += tn_dot(nf, gqkv)
        gnf = nt_dot(gqkv, w_ref[:, :3 * D])
        sums_scr[0] += fold8(gnf * xh1)
        sums_scr[2] += fold8(gnf)
        eg = gnf * gain1
        gtok = gmix + r1 * (eg - jnp.mean(eg, axis=1, keepdims=True) - xh1 * jnp.mean(eg * xh1, axis=1, keepdims=True))
        for h in range(2):
            part = gtok[h * SL:(h + 1) * SL]
            hi_ = part.astype(bf16)
            g_scr[b0 + h, :SL, :] = hi_
            g_scr[b0 + h, SL:, :] = (part - hi_.astype(f32)).astype(bf16)
        return 0

    lax.fori_loop(0, nsup, body, 0)

    tri_l = (jnp.where(ci < ri, 1.0, 0.0) - jnp.where(ri == ci, 256.0, 0.0)).astype(bf16)
    cif = ci.astype(f32)

    def unpack(t, _):
        bt = bin_smem[t]
        st = start_smem[t]
        col = nt_dot(tri_l, jnp.broadcast_to(o_ref[pl.ds(t, 1), :], (SL, SL)).astype(bf16))
        pt = jnp.where(col + (st + 256).astype(f32) == cif, 1.0, 0.0).astype(bf16)
        gtok_ref[t] = nn_dot(jnp.concatenate([pt, pt], axis=1), g_scr[bt])
        return 0

    lax.fori_loop(0, NT, unpack, 0)

    fin = [jnp.sum(sums_scr[k], axis=0, keepdims=True) for k in range(8)]
    gsm = jnp.concatenate([gpart_ref[:64, :]] + fin + [gpart_ref[72:73, :], jnp.zeros((55, D), f32)], axis=0).astype(bf16)
    eye = jnp.where(iota((D, D), 0) == iota((D, D), 1), 1.0, 0.0).astype(bf16)
    smt = nt_dot(eye, gsm)
    bup = jnp.sum(bup_scr[...], axis=0, keepdims=True).astype(bf16)
    dsel = iota((SL, FF), 0) == iota((SL, FF), 1) // 8
    bup_m = jnp.where(dsel, jnp.broadcast_to(bup, (SL, FF)), jnp.zeros((SL, FF), bf16))
    rep = jnp.where(iota((SL, FF), 0) == 80 + iota((SL, FF), 1) % 8, 1.0, 0.0).astype(bf16)
    bup_d = nt_dot(bup_m, rep)
    even = jnp.where(iota((D, SL), 0) == 2 * iota((D, SL), 1), 1.0, 0.0).astype(bf16)
    smt = (smt + nn_dot(even, bup_d.astype(bf16))).astype(bf16)
    gwd_t = [nt_dot(eye, gwd_scr[:, c * D:(c + 1) * D].astype(bf16)).astype(bf16) for c in range(4)]
    pr = iota((D, D), 0)
    pc = iota((D, D), 1)
    pd, prr = pr // 32, pr % 32
    want = jnp.where(prr < 18, (prr % 9) * 16 + pd * 2 + prr // 9, jnp.where(prr < 26, 144 + pd * 8 + prr - 18, -1))
    perm = jnp.where(want == pc, 1.0, 0.0).astype(bf16)
    sm_pad = jnp.zeros((16, SL), bf16)
    tail = jnp.zeros((48, D), bf16)
    for qn in range(16):
        r16 = slice(qn * 16, qn * 16 + 16)
        parts = [gw_scr[r16, bb * D:(bb + 1) * D].astype(bf16) for bb in range(8)]
        parts.append(jnp.concatenate([smt[r16], sm_pad], axis=1))
        o = (qn % 4) * 64
        parts.append(gwd_t[qn // 4][o:o + 64])
        parts.append(tail)
        gs_ref[qn] = nn_dot(perm, jnp.concatenate(parts, axis=0)).astype(bf16)


def encoder(caps, nt, o32, tok, w, wd, sm, r, gpart):
    rtot = sum(caps)
    vm = pl.BlockSpec(memory_space=pltpu.VMEM)
    return pl.pallas_call(
        functools.partial(encoder_kernel, caps),
        out_shape=(jax.ShapeDtypeStruct((NT, SL, D), f32), jax.ShapeDtypeStruct((rtot, D), bf16),
                   jax.ShapeDtypeStruct((16, D, D), bf16)),
        in_specs=[pl.BlockSpec(memory_space=pltpu.SMEM)] + [vm] * 7,
        out_specs=(vm, vm, vm),
        scratch_shapes=[
            pltpu.VMEM((NT, SL, D), f32), pltpu.VMEM((NT, SL, SL), f32), pltpu.VMEM((NT, 8, SL), f32),
            pltpu.VMEM((NT, 2 * SL, D), bf16), pltpu.VMEM((D, 2048), f32), pltpu.VMEM((D, FF), f32),
            pltpu.VMEM((8, 8, D), f32), pltpu.VMEM((8, FF), f32), pltpu.VMEM((NT, SL), f32),
            pltpu.VMEM((2 * SL, 768), bf16), pltpu.VMEM((2 * SL, 768), bf16), pltpu.VMEM((NT, 2 * SL), f32),
            pltpu.SMEM((NT,), i32), pltpu.SMEM((NT,), i32),
        ],
        compiler_params=pltpu.CompilerParams(vmem_limit_bytes=VMEM_LIMIT),
        name="encoder_fwd_bwd",
    )(nt, o32, tok, w, wd, sm, r, gpart)


def scatter_kernel(
    caps, gs_ref, s_ref, slab_out, rows_out,
    got1, sum1, got2, sum2, got3, sum3, got4, s_sem, r_sem, s1, r1, s2, r2, s3, r3, s4, r4, own_sem,
):
    me = Place()
    base = bases(caps)
    most, room = decode_room(caps)
    for i in range(8):
        rows_out[i] = jnp.zeros((room, D), bf16)
    barrier, count = me.greet()
    pl.semaphore_wait(barrier, count)

    step1 = []
    for x in (1, 3, 0, 2):
        c = remote(gs_ref.at[x, 1 - me.core], got1.at[x], s1.at[x], r1.at[x], me.sibling())
        c.start()
        step1.append((x, c))
    for k in (4, 3, 5, 2, 6, 1, 7, 0):
        for j in range(8):
            part = s_ref.at[pl.ds(base[j], caps[j])]
            there = rows_out.at[me.seq, pl.ds(0, caps[j])]
            if k == 0:
                @pl.when(me.seq == j)
                def _():
                    pltpu.make_async_copy(part, there, own_sem).start()
            else:
                @pl.when((me.seq + k) % 8 == j)
                def _():
                    remote(part, there, s_sem.at[k], r_sem.at[k], me.seq_peer(k)).start()

    for x, c in step1:
        c.wait()
        for z in range(4):
            for y in range(4):
                total = gs_ref[x, me.core, 4 * z + y].astype(f32) + got1[x, 4 * z + y].astype(f32)
                if x < 2:
                    sum1[0, z, x % 2, y] = total.astype(bf16)
                else:
                    sum1[1, y, x % 2, z] = total.astype(bf16)
    first = (me.z, me.y)
    second = (me.y, me.z)
    peers = (me.z_peer, me.y_peer)
    step2 = []
    for k in (2, 1, 3):
        for h in range(2):
            c = remote(sum1.at[h, (first[h] + k) % 4], got2.at[h, k - 1], s2.at[h, k - 1], r2.at[h, k - 1], peers[h](k))
            c.start()
            step2.append(c)
    for c in step2:
        c.wait()
    for h in range(2):
        for x2 in range(2):
            for o in range(4):
                total = sum1[h, first[h], x2, o].astype(f32)
                for k in range(3):
                    total = total + got2[h, k, x2, o].astype(f32)
                sum2[h, o, x2] = total.astype(bf16)
    step3 = []
    for k in (2, 1, 3):
        for h in range(2):
            c = remote(sum2.at[h, (second[h] + k) % 4], got3.at[h, k - 1], s3.at[h, k - 1], r3.at[h, k - 1], peers[1 - h](k))
            c.start()
            step3.append(c)
    for c in step3:
        c.wait()
    for h in range(2):
        for x2 in range(2):
            total = sum2[h, second[h], x2].astype(f32)
            for k in range(3):
                total = total + got3[h, k, x2].astype(f32)
            sum3[2 * h + x2] = total.astype(bf16)
    step4 = []
    for k in (2, 1, 3):
        c = remote(sum3.at[(me.x + k) % 4], got4.at[k - 1], s4.at[k - 1], r4.at[k - 1], me.x_peer(k))
        c.start()
        step4.append(c)
    for c in step4:
        c.wait()
    total = sum3[me.x].astype(f32)
    for k in range(3):
        total = total + got4[k].astype(f32)
    slab_out[...] = total

    for j in range(8):
        @pl.when(me.seq == j)
        def _():
            here = rows_out.at[0, pl.ds(0, caps[j])]
            for k in range(1, 8):
                pltpu.make_async_copy(here, here, r_sem.at[k]).wait()
            pltpu.make_async_copy(here, here, own_sem).wait()
            for k in range(1, 8):
                there = s_ref.at[pl.ds(base[(j + k) % 8], caps[(j + k) % 8])]
                pltpu.make_async_copy(there, there, s_sem.at[k]).wait()


def scatter(caps, gs, s, cid):
    dma = pltpu.SemaphoreType.DMA
    most, room = decode_room(caps)
    return pl.pallas_call(
        functools.partial(scatter_kernel, caps),
        out_shape=(jax.ShapeDtypeStruct((32, D), f32), jax.ShapeDtypeStruct((8, room, D), bf16)),
        in_specs=[vmem()] * 2,
        out_specs=(vmem(),) * 2,
        scratch_shapes=[
            pltpu.VMEM((4, 16, 32, D), bf16), pltpu.VMEM((2, 4, 2, 4, 32, D), bf16),
            pltpu.VMEM((2, 3, 2, 4, 32, D), bf16), pltpu.VMEM((2, 4, 2, 32, D), bf16),
            pltpu.VMEM((2, 3, 2, 32, D), bf16), pltpu.VMEM((4, 32, D), bf16), pltpu.VMEM((3, 32, D), bf16),
            dma((8,)), dma((8,)), dma((4,)), dma((4,)), dma((2, 3)), dma((2, 3)), dma((2, 3)), dma((2, 3)),
            dma((3,)), dma((3,)), dma,
        ],
        compiler_params=pltpu.CompilerParams(collective_id=cid, has_side_effects=True, vmem_limit_bytes=VMEM_LIMIT),
        name="scatter_and_exchange",
    )(gs, s)


def decode_kernel(
    caps, len_ref, vis_ref, rows_ref, sm_ref, slab_ref,
    dec_out, gain_out, shift_out, wq_out, wo_out, wu_out, wd_out, bias_out, up_out, mask_out, te_out,
    rows_scr,
):
    seq = lax.axis_index("seq")
    most, room = decode_room(caps)
    valid, shown = mask_rows(len_ref, vis_ref)
    v8, s8 = part_lanes(valid, shown, seq)
    stack = jnp.concatenate(
        [part_ranks(v8 * s8), v8 * (1.0 - s8), v8, jnp.zeros((SL - 24, PART), f32)], axis=0
    )
    cols = stack.T
    steps = sm_ref[pl.ds(pl.multiple_of(TE + 8 * seq, 8), 8), :]
    extra = jnp.concatenate([sm_ref[MASK : MASK + 1, :], steps, jnp.zeros((7, D), f32)], axis=0).astype(bf16)
    lane = iota((PART, room), 1)
    step_lane = most + 1 + (iota((PART, room), 0) % 16) // 2
    lane_rank = (lane - PART).astype(f32)
    for i in range(8):
        hit = (cols[:, i : i + 1] == lane_rank) & (lane < most)
        hidden = (lane == most) & (cols[:, 8 + i : 9 + i] > 0.0)
        timed = (lane == step_lane) & (cols[:, 16 + i : 17 + i] > 0.0)
        lhs = one_zero(hit | hidden | timed).astype(bf16)
        rows_scr[...] = rows_ref[i]
        rows_scr[most : most + 16, :] = extra
        got = nn_dot(lhs, rows_scr[...]).astype(bf16)
        dec_out[:, 8 * i : 8 * i + 8] = got.reshape(MICRO, 8, 16, D)

    slab = slab_ref[...]
    r, c = iota((SL, SL), 0), iota((SL, SL), 1)
    small = []
    for f in range(2):
        one = slice(f, f + 1)
        for b in range(3):
            wq_out[one, b * D : (b + 1) * D] = slab[9 * f + b : 9 * f + b + 1]
        wo_out[one, :] = slab[9 * f + 3 : 9 * f + 4]
        for b in range(4):
            wu_out[one, b * D : (b + 1) * D] = slab[9 * f + 4 + b : 9 * f + 5 + b]
        row = jnp.broadcast_to(slab[9 * f + 8 : 9 * f + 9, :SL], (SL, SL))
        small.append(jnp.sum(jnp.where(r == c, row, 0.0), axis=1, keepdims=True))
    wd_out[...] = slab[18:26]
    small = jnp.concatenate(small, axis=1)
    te_out[...] = small[TE : TE + 64]
    gain_out[...] = small[GAIN : GAIN + 2]
    shift_out[...] = small[SHIFT : SHIFT + 2]
    bias_out[...] = small[BIAS : BIAS + 4]
    mask_out[...] = small[MASK : MASK + 1]
    up_out[...] = slab[8:9, UP : UP + 8]


def decode(caps, lengths, visible, rows, sm, slab):
    most, room = decode_room(caps)
    s = jax.ShapeDtypeStruct
    return pl.pallas_call(
        functools.partial(decode_kernel, caps),
        out_shape=(
            s((MICRO, TRAJ, 16, D), bf16), s((2, 2), f32), s((2, 2), f32), s((2, 3 * D), f32), s((2, D), f32),
            s((2, FF), f32), s((8, D), f32), s((4, 2), f32), s((1, 8), f32), s((1, 2), f32), s((64, 2), f32),
        ),
        in_specs=[vmem()] * 5,
        out_specs=(vmem(),) * 11,
        scratch_shapes=[pltpu.VMEM((room, D), bf16)],
        compiler_params=pltpu.CompilerParams(vmem_limit_bytes=VMEM_LIMIT),
        name="decode",
    )(lengths, visible, rows, sm, slab)


def per_device(
    tokens, lengths, visible, norm_gains, norm_biases, w_qkv, w_out, w_up, w_down, proj_biases, up_bias, mask_token,
    time_embed, dec_grad,
):
    lengths, visible = lengths[:, 0], visible[:, 0]
    tok = tokens.reshape(NT, SL, D)
    dg = dec_grad[:, 0]
    small = jnp.concatenate(
        [time_embed.T, norm_gains.T, norm_biases.T, proj_biases.T, mask_token[:, None], jnp.zeros((2, 7), bf16)], axis=1
    )
    ups = jnp.concatenate([up_bias[None], jnp.zeros((1, 8), bf16)], axis=0)
    small = jnp.concatenate([small, ups, jnp.zeros((2, 40), bf16)], axis=1)
    w, wd, sm, rows, opened, counts, sums = gather(
        CAPS, lengths, visible, dg, w_qkv, w_out, w_up, w_down, small, 0
    )

    def rest(caps, rows, cid):
        gtok, s, gs = encoder(caps, counts, opened, tok, w, wd, sm, rows, sums)
        slab, back = scatter(caps, gs.reshape(4, 2, 16, 32, D), s, cid)
        return (gtok,) + tuple(decode(caps, lengths, visible, back, sm, slab))

    def roomy():
        return rest(FULL, exchange(FULL, lengths, visible, dg, 1), 2)

    outs = lax.cond(jnp.max(sm[FLAG]) > 0.0, roomy, lambda: rest(CAPS, rows, 3))
    gtok, dec, gain, shift, wq, wo, wu, wdn, bias, up, mask, te = outs
    return (
        dec.reshape(MICRO, 1, TRAJ, 16, D), gtok.reshape(MICRO, 1, 8, SL, D), gain, shift, wq, wo, wu, wdn, bias,
        up.reshape(8), mask.reshape(2), te,
    )


def solution(mesh):
    everyone = ("seq", "dp")
    return jax.shard_map(
        per_device,
        mesh=mesh,
        in_specs=(
            P(None, "dp", "seq", None, None), P(None, "dp", None), P(None, "dp", None, None), P(None, everyone),
            P(None, everyone), P(everyone, None), P(everyone, None), P(everyone, None), P(everyone, None),
            P(None, everyone), P(everyone), P(everyone), P(None, everyone), P(None, "dp", None, "seq", None),
        ),
        out_specs=(
            P(None, "dp", None, "seq", None), P(None, "dp", "seq", None, None), P(None, everyone), P(None, everyone),
            P(everyone, None), P(everyone, None), P(everyone, None), P(everyone, None), P(None, everyone), P(everyone),
            P(everyone), P(None, everyone),
        ),
        check_vma=False,
    )
```

time: 815 us -> 113 us (0.14); the launches traced: 804 us -> 111 us
  blocking collectives: 257 us -> 0 us
  matrix products: 137 us -> 0 us
  local copies, waits for them, and re-layouts: 131 us -> 7.08 us
  Pallas kernels: 0 us -> 101 us
  starting transfers between devices: 100 us -> 0 us
  waiting for transfers between devices: 83.9 us -> 0 us
  other arithmetic: 79.6 us -> 0.6 us
  between operations: 17.1 us -> 1.35 us
    all_gather x4 -> x0, blocking collectives: 192 us -> none  [the longest x1 55.7 us: fetch_weights(): lax.all_gather(w_down, SEQ_DP, axis=0, tiled=True)]
    dot_general x72 -> x0, matrix products: 137 us -> none  [the longest x4 17.2 us: per_device(): jnp.einsum('tpd,fd->tpf', grad_encoded_low, weight_down, preferred_elemen...]
    pallas_call x0 -> x4, Pallas kernels: none -> 101 us  [the longest x1 42.6 us: encoder(): pl.pallas_call(functools.partial(encoder_kernel, caps), out_shape=(jax.Sh...]
    all_to_all x22 -> x0, starting transfers between devices: 100 us -> none  [the longest x7 38.4 us: summed_rows(): return jnp.sum(lax.all_to_all(own, far, 0, 0, tiled=True), axis=0)]
    all_to_all x22 -> x0, waiting for transfers between devices: 83.9 us -> none  [the longest x7 24.8 us: summed_on_arrival(): lax.all_to_all(parts, axis, split_axis=0, concat_axis=0, tiled=True)]
    unnamed x1 -> x0, blocking collectives: 64.9 us -> none
    reduce_sum x44 -> x0, other arithmetic: 42.2 us -> none  [the longest x4 7.74 us: per_device(): grad_qkv_sums = jnp.sum(grad_qkv_low.astype(f32), axis=(0, 1))]
    another operation x69 -> x1, local copies, waits for them, and re-layouts: 24.1 us -> 0.01 us  [the longest x3 8.93 us: in_blocks(): array.reshape(*dims[:dim], devices, dims[dim] // devices, *dims[dim + 1:])]
  transfers between devices with their start and end apart: 23 -> 0, of which waited for: 15 -> 0; matrix products, arithmetic and copies ran while one was open for 19% -> 0% of each run, Pallas kernels for 0% -> 0%
where the time goes in v1:
time: 113 us; the launch traced here: 111 us
  Pallas kernels  101 us (89%)
  local copies, waits for them, and re-layouts  7.08 us (6%)
  between operations  1.35 us (1%)
    pallas_call x1, Pallas kernels, encoder(): pl.pallas_call(functools.partial(encoder_kernel, caps), out_shape=(jax.Sh...  42.6 us
    pallas_call x1, Pallas kernels, gather(): pl.pallas_call(functools.partial(gather_kernel, caps), out_shape=(jax.Sha...  27.6 us
    pallas_call x1, Pallas kernels, scatter(): pl.pallas_call(functools.partial(scatter_kernel, caps), out_shape=(jax.Sh...  23.7 us
    pallas_call x1, Pallas kernels, decode(): pl.pallas_call(functools.partial(decode_kernel, caps), out_shape=(s((MICR...  7.35 us
    unnamed x8, local copies, waits for them, and re-layouts  4.39 us

profile of v1, /device:TPU:0, one launch (start us, length us, event | category | flops | bytes accessed | tf_op | source)
XLA Modules:
  0.0 110.9 jit_solution(11860304644645162742)
XLA Ops:
  0.6 0.0 copy-start
  0.7 0.0 copy-start.2
  0.7 0.9 copy.26
  1.6 0.8 copy.27
  2.3 0.7 concatenate.6
  3.0 0.8 copy.28
  3.8 1.3 %concatenate.7.small_ref = bf16[2,128]{1,0:T(2,128)(2,1)} concatenate(bf16[2,64]{1,0:T(2,128)(2,1)} %bitcast.28, bf16[2,2]{1,0:T(2,128)(2,1)S(1)} %bitcast.30, bf16[2,2]{1,0:T(2,128)(2,1)S(1)} %bitcast.31, bf16[2,4]{1,0:T(2,128)(2,1)} %bitcast.29, bf16[2,1]{1,0:T(2,128)(2,1)S(1)} %copy.28, bf16[2,7]{1,0:T(2,128)(2,1)S(1)} %broadcast.6, bf16[2,8]{1,0:T(2,128)(2,1)S(1)} %concatenate.6, ...), dimensions={1} | concatenate | bytes 1024 | tf_op jit(solution)/shard_map/concatenate | solution.py:888
  5.0 27.6 %gather_and_exchange.1 = (bf16[256,2048]{1,0:T(8,128)(2,1)S(1)}, bf16[1024,256]{1,0:T(8,128)(2,1)}, f32[128,256]{1,0:T(8,128)S(1)}, bf16[1216,256]{1,0:T(8,128)(...) custom-call(s32[4,64]{1,0:T(4,128)} %bitcast.25, s32[4,64,128]{2,1,0:T(8,128)} %bitcast.20, ...), custom_call_target="tpu_custom_call" | custom-call | tf_op jit(solution)/shard_map/gather_and_exchange/pallas_call | solution.py:367
  32.6 0.6 slice_reduce_fusion
  33.9 0.0 copy-done
  33.9 0.0 copy-done.2
  33.9 74.3 %conditional.1 = (f32[32,128,256]{2,1,0:T(8,128)}, bf16[4,64,16,256]{3,2,1,0:T(8,128)(2,1)}, f32[2,2]{1,0:T(2,128)}, f32[2,2]{1,0:T(2,128)}, f32[2,768]{1,0:T(2,...) conditional(s32[]{:T(128)} %convert_element_type.3, ...), branch_computations={%region_1.0_spmd, %region_2.0_spmd} | conditional | bytes 10506448 | solution.py:901
  33.9 42.6 %encoder_fwd_bwd.2 = (f32[32,128,256]{2,1,0:T(8,128)}, bf16[1216,256]{1,0:T(8,128)(2,1)}, bf16[16,256,256]{2,1,0:T(8,128)(2,1)}) custom-call(s32[8,128]{1,0:T(8,128)} %get-tuple-element.40.nt_ref, f32[32,128]{1,0:T(8,128)S(1)} %get-tuple-element.41.o_ref, bf16[32,128,256]{2,1,0:T(8,128)(2,1)} %get-tuple-element.42.tok_ref, ...), custom_call_target="tpu_custom_call" | custom-call | tf_op jit(solution)/shard_map/cond/branch_0_fun/encoder_fwd_bwd/pallas_call | solution.py:677
  76.5 0.0 copy-start.4
  76.5 23.7 %scatter_and_exchange.2 = (f32[32,256]{1,0:T(8,128)}, bf16[8,384,256]{2,1,0:T(8,128)(2,1)}) custom-call(bf16[4,2,16,32,256]{4,3,2,1,0:T(8,128)(2,1)} %bitcast.24, bf16[1216,256]{1,0:T(8,128)(2,1)} %get-tuple-element.52.s_ref), custom_call_target="tpu_custom_call" | custom-call | tf_op jit(solution)/shard_map/cond/branch_0_fun/scatter_and_exchange/pallas_call | solution.py:793
  100.3 0.0 copy-done.4
  100.3 7.3 %decode.2 = (bf16[4,64,16,256]{3,2,1,0:T(8,128)(2,1)}, f32[2,2]{1,0:T(2,128)}, f32[2,2]{1,0:T(2,128)}, f32[2,768]{1,0:T(2,128)}, f32[2,256]{1,0:T(2,128)}, /*ind...) custom-call(s32[4,64]{1,0:T(4,128)S(1)} %copy-done.4, ...), custom_call_target="tpu_custom_call" | custom-call | tf_op jit(solution)/shard_map/cond/branch_0_fun/decode/pallas_call | solution.py:863
  108.2 1.3 %copy.29 = f32[4,2]{0,1:T(2,128)} copy(f32[4,2]{1,0:T(4,128)} %get-tuple-element.150) | data formatting | bytes 64
  109.5 1.4 %copy.30 = f32[64,2]{0,1:T(2,128)} copy(f32[64,2]{1,0:T(8,128)} %get-tuple-element.153) | data formatting | bytes 1024
  (2 shorter events, 0.0 us)
Async XLA Ops:
  0.6 33.2 %copy-start = (bf16[4,1,64,16,256]{4,3,2,1,0:T(8,128)(2,1)S(1)}, bf16[4,1,64,16,256]{4,3,2,1,0:T(8,128)(2,1)}, u32[]{:S(2)}) copy-start(bf16[4,1,64,16,256]{4,3,2,1,0:T(8,128)(2,1)} %param.29) | copy-start | bytes 6291460
  0.7 33.2 %copy-start.2 = (s32[4,1,64,128]{3,2,1,0:T(8,128)S(1)}, s32[4,1,64,128]{3,2,1,0:T(8,128)}, u32[]{:S(2)}) copy-start(s32[4,1,64,128]{3,2,1,0:T(8,128)} %param.18) | copy-start | bytes 393220
  76.5 23.8 %copy-start.4 = (s32[4,64]{1,0:T(4,128)S(1)}, s32[4,64]{1,0:T(4,128)}, u32[]{:S(2)}) copy-start(s32[4,64]{1,0:T(4,128)} %get-tuple-element.49.len_ref) | copy-start | bytes 3076 | tf_op jit(solution)/shard_map/cond

commit v2 on v1

v2 whole, which is shorter than its diff:
```python
import functools

import jax
import jax.numpy as jnp
from jax import lax
from jax.experimental import pallas as pl
from jax.experimental.pallas import tpu as pltpu
from jax.sharding import PartitionSpec as P

f32, bf16, i32 = jnp.float32, jnp.bfloat16, jnp.int32
EPS = 1e-5
BIG = 1e30
D, FF, SL, MICRO, TRAJ = 256, 1024, 128, 4, 64
NT = 32
PART = 512
GELU_A = 0.7978845608028654
GELU_B = 0.044715
CAPS, NBINS = (304, 240, 192, 160, 128, 80, 64, 48), 8
FULL, NFULL = (PART,) * 8, NT
MESH = pl.DeviceIdType.MESH
VMEM_LIMIT = 30 * 2**20
VMEM_MOST = 56 * 2**20

TE, GAIN, SHIFT, BIAS, MASK, UP, FLAG = 0, 64, 66, 68, 72, 80, 96


def nt_dot(a, b):
    return lax.dot_general(a, b, (((1,), (1,)), ((), ())), preferred_element_type=f32)


def nn_dot(a, b):
    return lax.dot_general(a, b, (((1,), (0,)), ((), ())), preferred_element_type=f32)


def tn_dot(a, b):
    return lax.dot_general(a, b, (((0,), (0,)), ((), ())), preferred_element_type=f32)


def iota(shape, dim):
    return lax.broadcasted_iota(i32, shape, dim)


def one_zero(cond):
    return jnp.where(cond, 1.0, 0.0)


def fold8(v):
    n = v.shape[0] // 8
    return jnp.sum(v.reshape(n, 8, v.shape[1]), axis=0)


def bases(caps):
    out, at = [], 0
    for c in caps:
        out.append(at)
        at += c
    return out


def decode_room(caps):
    most = max(caps)
    return most, -(-(most + 16) // SL) * SL


class Place:
    def __init__(self):
        self.seq = lax.axis_index("seq")
        self.dp = lax.axis_index("dp")
        self.x, self.core = self.seq // 2, self.seq % 2
        self.z, self.y = self.dp // 4, self.dp % 4

    def at(self, x, y, z):
        return (2 * x + self.core, z * 4 + y)

    def seq_peer(self, k):
        return ((self.seq + k) % 8, self.dp)

    def y_peer(self, k):
        return self.at(self.x, (self.y + k) % 4, self.z)

    def z_peer(self, k):
        return self.at(self.x, self.y, (self.z + k) % 4)

    def sibling(self):
        return (self.seq + 1 - 2 * self.core, self.dp)

    def greet(self, everyone=True):
        peers = [self.seq_peer(k) for k in range(1, 8)]
        if everyone:
            for dx in range(4):
                for d in range(1, 4):
                    peers.append(self.at((self.x + dx) % 4, (self.y + d) % 4, self.z))
                    peers.append(self.at((self.x + dx) % 4, self.y, (self.z + d) % 4))
        barrier = pltpu.get_barrier_semaphore()
        for peer in peers:
            pl.semaphore_signal(barrier, inc=1, device_id=peer, device_id_type=MESH)
        return barrier, len(peers)


def remote(src, dst, send_sem, recv_sem, peer):
    return pltpu.make_async_remote_copy(
        src_ref=src, dst_ref=dst, send_sem=send_sem, recv_sem=recv_sem, device_id=peer, device_id_type=MESH
    )


def arrived(ref, sem):
    pltpu.make_async_copy(ref, ref, sem).wait()


def vmem():
    return pl.BlockSpec(memory_space=pltpu.VMEM)


def hbm():
    return pl.BlockSpec(memory_space=pltpu.HBM)


def smem():
    return pl.BlockSpec(memory_space=pltpu.SMEM)


def mask_rows(len_ref, vis_ref):
    eye = one_zero(iota((TRAJ, TRAJ), 0) == iota((TRAJ, TRAJ), 1)).astype(bf16)
    step = (iota((TRAJ, SL), 1) // 2).astype(f32)
    valid, shown = [], []
    for m in range(MICRO):
        row = jnp.broadcast_to(len_ref[m : m + 1, :].astype(f32), (SL, TRAJ)).astype(bf16)
        valid.append(one_zero(step < nt_dot(eye, row)))
        shown.append(one_zero(vis_ref[m] > 0))
    return jnp.concatenate(valid, axis=0), jnp.concatenate(shown, axis=0)


def part_lanes(valid, shown, part):
    n = MICRO * TRAJ
    pick = one_zero(iota((SL, PART), 0) == 16 * part + iota((SL, PART), 1) % 16).astype(bf16)
    row, lane = iota((n, PART), 0), iota((n, PART), 1)
    mine = (row // TRAJ == lane // SL) & (row % 8 == (lane % SL) // 16)
    group = one_zero((iota((16, n), 1) % TRAJ) // 8 == iota((16, n), 0)).astype(bf16)

    def lanes(mask):
        spread = nn_dot(mask.astype(bf16), pick)
        return nn_dot(group, jnp.where(mine, spread, 0.0).astype(bf16))[:8]

    return lanes(valid), lanes(shown)


def part_ranks(open_lanes):
    tri = one_zero(iota((PART, PART), 0) < iota((PART, PART), 1)).astype(bf16)
    rows = jnp.concatenate([open_lanes, jnp.zeros((8, PART), f32)], axis=0).astype(bf16)
    return nn_dot(rows, tri)[:8]


def prepare_part(caps, seq, valid, shown, rank_scr, ext_scr, cols_out):
    most, _ = decode_room(caps)
    v8, s8 = part_lanes(valid, shown, seq)
    rank = part_ranks(v8 * s8)
    rank_scr[...] = jnp.where(v8 * s8 > 0.0, rank, -1.0)
    lane_step = (iota((8, PART), 1) % 16) // 2
    step_row = iota((8, PART), 0)
    for i in range(8):
        v = v8[i : i + 1, :]
        steps = jnp.where(lane_step == step_row, jnp.broadcast_to(v, (8, PART)), 0.0)
        hidden = jnp.where(step_row == 0, jnp.broadcast_to(v * (1.0 - s8[i : i + 1, :]), (8, PART)), 0.0)
        ext_scr[i] = jnp.concatenate([steps, hidden], axis=0)
    first = jnp.where(v8 > 0.0, jnp.where(s8 > 0.0, rank, float(most)), -1.0)
    second = jnp.where(v8 > 0.0, (most + 1 + lane_step).astype(f32), -1.0)
    cols_out[...] = jnp.concatenate([first, second, jnp.zeros((SL - 16, PART), f32)], axis=0).T


def plan_bins(caps, nbins, opened, base_scr, bin_scr, pos_scr, srct_scr, seg_out, bins_out, count_out, slot_out):
    n_rep = nn_dot(opened.astype(bf16), jnp.ones((SL, SL), bf16))
    at = [jnp.full((1, SL), float(k), f32) for k in range(3)]
    used = [jnp.zeros((1, SL), f32) for _ in range(3)]
    last = jnp.zeros((1, SL), f32)
    for t in range(NT):
        n = n_rep[t : t + 1]
        fits = [u + n <= float(SL) for u in used]
        none = jnp.logical_not(fits[0] | fits[1] | fits[2])
        used = [jnp.where(none, u, v) for u, v in zip(used[1:] + [jnp.zeros((1, SL), f32)], used)]
        at = [jnp.where(none, a, b) for a, b in zip(at[1:] + [at[2] + 1.0], at)]
        take = [fits[0], fits[1] & jnp.logical_not(fits[0])]
        take.append(jnp.logical_not(take[0] | take[1]))
        bin_now = jnp.where(take[0], at[0], jnp.where(take[1], at[1], at[2]))
        off = jnp.where(take[0], used[0], jnp.where(take[1], used[1], used[2]))
        used = [jnp.where(f, u + n, u) for f, u in zip(take, used)]
        last = jnp.maximum(last, bin_now)
        base_scr[t : t + 1, :] = bin_now * float(SL) + off
        bin_scr[t : t + 1, :] = bin_now
    ri, ci = iota((SL, SL), 0), iota((SL, SL), 1)
    within = nn_dot(opened.astype(bf16), one_zero(ri < ci).astype(bf16))
    base, bins = base_scr[...], bin_scr[...]
    pos = jnp.where(opened > 0.0, base + within, -1.0)
    pos_scr[...] = pos
    pad = jnp.zeros((SL - NT, SL), f32)
    slot_out[...] = jnp.concatenate([jnp.where(opened > 0.0, pos - bins * float(SL), -1.0), pad], axis=0).T
    lo = jnp.concatenate([base, pad], axis=0).T[:8]
    hi = jnp.concatenate([base + n_rep, pad], axis=0).T[:8]
    seg_out[...] = jnp.where(iota((8, SL), 0) == 0, lo, hi)
    bins_out[...] = jnp.concatenate([bins, pad], axis=0).T[:8].astype(i32)
    count_out[...] = jnp.broadcast_to(last + 1.0, (8, SL)).astype(i32)
    same = ri // 16 == ci // 16
    first = bases(caps)
    lane_blk = iota((NT, SL), 1) // 16
    src = jnp.ones((NT, SL), f32)
    for j in range(8):
        src = jnp.where(lane_blk == j, float(first[j] + 1), src)
    before = nn_dot(one_zero(iota((NT, NT), 1) < iota((NT, NT), 0)).astype(bf16), opened.astype(bf16))
    src = src + nn_dot(opened.astype(bf16), one_zero(same & (ri < ci)).astype(bf16))
    src = src + nn_dot(before.astype(bf16), one_zero(same).astype(bf16))
    big = jnp.floor(src * (1.0 / 256.0)) * 256.0
    srct_scr[...] = jnp.concatenate([big, src - big, jnp.zeros((SL - 2 * NT, SL), f32)], axis=0).T.astype(bf16)
    return one_zero(last[:, :1] + 1.0 > float(nbins))


def pack_tokens(nbins, tok_ref, pos_scr, srct_scr, seg_out, src_scr, x_out, src_out):
    m = 2 * SL
    row = iota((m, SL), 0).astype(f32)
    row_low = iota((m, m), 0).astype(f32).astype(bf16)
    one, zero = jnp.ones((m, m), bf16), jnp.zeros((m, m), bf16)
    lo, hi = seg_out[0:1, :], seg_out[1:2, :]
    lo2 = jnp.concatenate([lo[:, :NT], lo[:, :NT], lo[:, 2 * NT :]], axis=1)
    hi2 = jnp.concatenate([hi[:, :NT], hi[:, :NT], hi[:, 2 * NT :]], axis=1)

    def pair(s, _):
        here = pl.ds(pl.multiple_of(s * m, m), m)
        at = row + (s * m).astype(f32)
        total = jnp.zeros((m, D), f32)
        slots = jnp.zeros((m, SL), bf16)
        for t in range(0, NT, 2):
            local = jnp.concatenate([pos_scr[t : t + 1, :], pos_scr[t + 1 : t + 2, :]], axis=1) - (s * m).astype(f32)
            local = jnp.where((local >= 0.0) & (local < float(m)), local, -1.0)
            p = jnp.where(row_low == jnp.broadcast_to(local, (m, m)).astype(bf16), one, zero)
            slots = slots + (p[:, :SL] + p[:, SL:])
            total = total + nn_dot(p, tok_ref[t : t + 2].reshape(m, D))
        x_out[here, :] = total.astype(bf16)
        seg = (at >= lo2) & (at < hi2)
        src = jnp.sum(jnp.where(seg, nn_dot(slots, srct_scr[...]), 0.0), axis=1, keepdims=True)
        src = jnp.broadcast_to(src, (m, SL))
        src_scr[here, :] = src
        src_out[pl.ds(pl.multiple_of(s * 16, 16), 16), :] = jnp.concatenate([src[:SL].T[:8], src[SL:].T[:8]], axis=0)
        return 0

    lax.fori_loop(0, nbins // 2, pair, 0)


def pack_received(caps, nbins, r_ref, src_scr, ge_out):
    total = sum(caps)
    m = 2 * SL
    lane = iota((m, SL), 1).astype(f32)

    def one(s, _):
        here = pl.ds(pl.multiple_of(s * m, m), m)
        src = src_scr[here, :]
        got = jnp.zeros((m, D), f32)
        for c in range(0, total, 256):
            wide = min(256, total - c)
            hit = [
                one_zero(src[:, :w] == lane[:, :w] + float(c + d + 1))
                for d in range(0, wide, SL) for w in [min(SL, wide - d)]
            ]
            got = got + nn_dot(jnp.concatenate(hit, axis=1).astype(bf16), r_ref[c : c + wide, :])
        ge_out[here, :] = got.astype(bf16)
        return 0

    lax.fori_loop(0, nbins // 2, one, 0)


def pack_part(caps, me, k, dg_ref, rank_scr, ext_scr, buf):
    most = max(caps)
    owner = (me.seq + k) % 8
    hit = one_zero(rank_scr[pl.ds(owner, 1), :] == iota((most, PART), 0).astype(f32))
    lhs = jnp.concatenate([hit, ext_scr[owner]], axis=0).astype(bf16)
    first = pl.multiple_of(owner * 8, 8)
    parts = [dg_ref[m, pl.ds(first, 8)].reshape(SL, D) for m in range(MICRO)]
    got = nn_dot(lhs, jnp.concatenate(parts, axis=0))
    buf[k] = got[:most].astype(bf16)
    return got[most:]


def send_parts(caps, me, buf, r_ref, sends, recvs):
    base = bases(caps)
    for j in range(8):
        @pl.when(me.seq == j)
        def _():
            there = r_ref.at[pl.ds(base[j], caps[j])]
            for k in (4, 3, 5, 2, 6, 1, 7):
                remote(buf.at[k, pl.ds(0, caps[j])], there, sends.at[k], recvs.at[j], me.seq_peer(k)).start()
            there[...] = buf[0, : caps[j]]


def finish_parts(caps, me, buf, r_ref, sends, recvs):
    base = bases(caps)
    for j in range(8):
        @pl.when(me.seq != j)
        def _():
            arrived(r_ref.at[pl.ds(base[j], caps[j])], recvs.at[j])

        @pl.when(me.seq == j)
        def _():
            for k in range(1, 8):
                arrived(buf.at[k, pl.ds(0, caps[j])], sends.at[k])


def part_scratch(caps, nbins):
    return [
        pltpu.VMEM((MICRO, TRAJ, 16, D), bf16),
        pltpu.VMEM((NT, SL, D), bf16),
        pltpu.SemaphoreType.DMA((2,)),
        pltpu.VMEM((MICRO * TRAJ, SL), f32),
        pltpu.VMEM((8, PART), f32),
        pltpu.VMEM((8, 16, PART), f32),
        pltpu.VMEM((8, max(caps), D), bf16),
        pltpu.VMEM((sum(caps), D), bf16),
        pltpu.SemaphoreType.DMA((8,)),
        pltpu.SemaphoreType.DMA((8,)),
        pltpu.VMEM((NT, SL), f32),
        pltpu.VMEM((NT, SL), f32),
        pltpu.VMEM((NT, SL), f32),
        pltpu.VMEM((SL, SL), bf16),
        pltpu.VMEM((nbins * SL, SL), f32),
    ]


def part_outs(caps, nbins):
    s = jax.ShapeDtypeStruct
    return (
        s((nbins * SL, D), bf16),
        s((nbins * SL, D), bf16),
        s((8, SL), f32),
        s((nbins * 8, SL), f32),
        s((SL, SL), f32),
        s((8, SL), i32),
        s((8, SL), i32),
        s((PART, SL), f32),
    )


class Parts:
    def __init__(self, caps, nbins, me, len_ref, vis_ref, dg_hbm, tok_hbm, outs, scratch):
        self.caps, self.nbins, self.me = caps, nbins, me
        self.len_ref, self.vis_ref, self.dg_hbm, self.tok_hbm = len_ref, vis_ref, dg_hbm, tok_hbm
        self.x, self.ge, self.seg, self.src, self.slot, self.bins, self.count, self.cols = outs
        (
            self.dg, self.tok, self.load_sem, self.open_scr, self.rank, self.ext, self.buf, self.r, self.sends,
            self.recvs, self.base_scr, self.bin_scr, self.pos, self.srct, self.src_scr,
        ) = scratch

    def load(self):
        self.loads = [
            pltpu.make_async_copy(self.dg_hbm, self.dg, self.load_sem.at[0]),
            pltpu.make_async_copy(self.tok_hbm, self.tok, self.load_sem.at[1]),
        ]
        for c in self.loads:
            c.start()

    def prepare(self):
        me = self.me
        valid, shown = mask_rows(self.len_ref, self.vis_ref)
        opened = valid * shown
        self.open_scr[...] = opened
        mine = [
            self.open_scr[pl.ds(pl.multiple_of(m * TRAJ + 8 * me.seq, 8), 8), :] for m in range(MICRO)
        ]
        over = plan_bins(
            self.caps, self.nbins, jnp.concatenate(mine, axis=0), self.base_scr, self.bin_scr, self.pos, self.srct,
            self.seg, self.bins, self.count, self.slot,
        )
        prepare_part(self.caps, me.seq, valid, shown, self.rank, self.ext, self.cols)
        return opened, over

    def send(self):
        sums = jnp.zeros((16, D), f32)
        for k in range(8):
            sums = sums + pack_part(self.caps, self.me, k, self.dg, self.rank, self.ext, self.buf)
        send_parts(self.caps, self.me, self.buf, self.r, self.sends, self.recvs)
        return sums

    def pack_tokens(self):
        pack_tokens(self.nbins, self.tok, self.pos, self.srct, self.seg, self.src_scr, self.x, self.src)

    def receive(self):
        finish_parts(self.caps, self.me, self.buf, self.r, self.sends, self.recvs)
        pack_received(self.caps, self.nbins, self.r, self.src_scr, self.ge)


def exchange_kernel(caps, nbins, len_ref, vis_ref, dg_hbm, tok_hbm, *refs):
    me = Place()
    barrier, count = me.greet(everyone=False)
    parts = Parts(caps, nbins, me, len_ref, vis_ref, dg_hbm, tok_hbm, refs[:8], refs[8:])
    parts.load()
    parts.prepare()
    for c in parts.loads:
        c.wait()
    pl.semaphore_wait(barrier, count)
    parts.send()
    parts.pack_tokens()
    parts.receive()


def exchange(caps, nbins, lengths, visible, dec_grad, tokens, cid):
    return pl.pallas_call(
        functools.partial(exchange_kernel, caps, nbins),
        out_shape=part_outs(caps, nbins),
        in_specs=[vmem(), vmem(), hbm(), hbm()],
        out_specs=(vmem(),) * 8,
        scratch_shapes=part_scratch(caps, nbins),
        compiler_params=pltpu.CompilerParams(collective_id=cid, has_side_effects=True, vmem_limit_bytes=VMEM_LIMIT),
        name="exchange_gradients",
    )(lengths, visible, dec_grad, tokens)


def gather_kernel(
    caps, nbins, dg_hbm, tok_hbm, *refs,
):
    me = Place()
    given, refs = refs[:12], refs[12:]
    w_out, wdn_out, sm_out, part_out, flag_out = refs[:5]
    refs = refs[5:]
    slabs, small, features, s1, r1, s2, r2, s3, r3, given_sem = refs[-22:-12]
    held = refs[-12:]
    len_ref, vis_ref, wq_ref, wo_ref, wu_ref, wd_ref, gain_ref, shift_ref, bias_ref, up_ref, mask_ref, te_ref = held
    loads = [pltpu.make_async_copy(a, b, given_sem.at[n]) for n, (a, b) in enumerate(zip(given, held))]
    for c in loads:
        c.start()
    barrier, count = me.greet()
    parts = Parts(caps, nbins, me, len_ref, vis_ref, dg_hbm, tok_hbm, refs[:8], refs[8:-22])
    parts.load()
    for c in loads:
        c.wait()
    opened, over = parts.prepare()
    half, x2 = me.x // 2, me.x % 2
    lines = (me.y, me.z)
    own = (me.z + half * (me.y - me.z), me.y + half * (me.z - me.y))

    n = MICRO * TRAJ
    group = one_zero((iota((16, n), 1) % TRAJ) // 8 == iota((16, n), 0)).astype(bf16)
    blk = one_zero(iota((SL, SL), 0) // 16 == iota((SL, SL), 1) // 16).astype(bf16)
    pairs = nn_dot(nn_dot(group, opened.astype(bf16)).astype(bf16), blk)
    lane_blk = iota((16, SL), 1) // 16
    room = jnp.zeros((16, SL), f32)
    for j in range(8):
        room = jnp.where(lane_blk == j, float(caps[j]), room)
    crowded = jnp.max(jnp.max(one_zero(pairs > room), axis=1, keepdims=True), axis=0, keepdims=True)
    over = jnp.maximum(over, crowded)

    small[...] = jnp.zeros_like(small)
    small[:, TE : TE + 64] = te_ref[...].astype(f32)
    small[:, BIAS : BIAS + 4] = bias_ref[...].astype(f32)
    small[0:1, UP : UP + 8] = up_ref[...].astype(f32)
    gains, shifts, masks = gain_ref[...].astype(f32), shift_ref[...].astype(f32), mask_ref[...].astype(f32)
    for f in range(2):
        for g in range(2):
            small[f : f + 1, GAIN + g : GAIN + g + 1] = gains[g : g + 1, f : f + 1]
            small[f : f + 1, SHIFT + g : SHIFT + g + 1] = shifts[g : g + 1, f : f + 1]
        small[f : f + 1, MASK : MASK + 1] = masks[:, f : f + 1]
    small[0:1, FLAG : FLAG + 1] = over
    extra = jnp.concatenate([small[...], jnp.zeros((2, SL), f32)], axis=1)
    rows = []
    for f in range(2):
        one = slice(f, f + 1)
        rows += [wq_ref[one, c : c + D].astype(f32) for c in range(0, 3 * D, D)]
        rows += [wo_ref[one, :].astype(f32)]
        rows += [wu_ref[one, c : c + D].astype(f32) for c in range(0, 4 * D, D)]
        rows += [extra[one]]
    slab = jnp.concatenate(rows + [wd_ref[...].astype(f32), jnp.zeros((6, D), f32)], axis=0)
    mine = slabs.at[half, me.core, own[0], own[1], x2]
    mine[...] = slab.astype(bf16)

    pl.semaphore_wait(barrier, count)
    step1 = []
    for d, dx in sorted(((d, dx) for d in range(4) for dx in range(4) if d or dx), key=lambda p: p[0] % 3 + p[1] % 3):
        peer = me.at((me.x + dx) % 4, (me.y + (1 - half) * d) % 4, (me.z + half * d) % 4)
        c = remote(mine, mine, s1.at[4 * d + dx], r1.at[half, own[1], x2], peer)
        c.start()
        step1.append(c)
    for c in parts.loads:
        c.wait()
    sums = parts.send()
    part_out[...] = jnp.zeros_like(part_out)
    part_out[pl.ds(pl.multiple_of(8 * me.seq, 8), 8), :] = sums[:8]
    part_out[MASK : MASK + 1, :] = sums[8:9]
    for h in range(2):
        line = slabs.at[h, me.core, lines[1 - h]]
        for o in range(4):
            for a in range(2):
                @pl.when((me.x != 2 * h + a) | (lines[h] != o))
                def _():
                    arrived(line.at[o, a], r1.at[h, o, a])

    step2, step3 = [], []
    for k in range(3):
        for h in range(2):
            line = slabs.at[h, me.core, lines[1 - h]]
            c = remote(line, line, s2.at[h, k], r2.at[h, k], (me.z_peer, me.y_peer)[h](k + 1))
            c.start()
            step2.append(c)
    for h in range(2):
        line = slabs.at[h, me.core, lines[1 - h]]
        c = remote(line, line, s3.at[h, 0], r3.at[h, 0], me.sibling())
        c.start()
        step3.append(c)
    parts.pack_tokens()
    for k in range(3):
        for h in range(2):
            step2[2 * k + h].wait()
            line = slabs.at[h, me.core, (lines[1 - h] + 3 - k) % 4]
            c = remote(line, line, s3.at[h, k + 1], r3.at[h, k + 1], me.sibling())
            c.start()
            step3.append(c)
    for c in step1:
        c.wait_send()

    pr, pc = iota((D, D), 0), iota((D, D), 1)
    want = jnp.where(
        pr < 144,
        ((pr % 16) // 2) * 32 + (pr % 2) * 9 + pr // 16,
        jnp.where(pr < 208, ((pr - 144) // 8) * 32 + 18 + (pr - 144) % 8, -1),
    )
    perm = one_zero(want == pc).astype(bf16)

    def place(core):
        for x in range(4):
            for z0 in range(2):
                at = 4 * x + 2 * core + z0
                chunk = []
                for z in (2 * z0, 2 * z0 + 1):
                    for y in range(4):
                        a, b = (z, y) if x < 2 else (y, z)
                        chunk.append(slabs[x // 2, core, a, b, x % 2])
                got = nn_dot(perm, jnp.concatenate(chunk, axis=0)).astype(bf16)
                r16 = pl.ds(pl.multiple_of(at * 16, 16), 16)
                for b in range(8):
                    w_out[r16, b * D : (b + 1) * D] = got[16 * b : 16 * b + 16]
                features[r16, :] = got[128:144, :SL]
                wdn_out[pl.ds(pl.multiple_of(at * 64, 64), 64), :] = got[144:208]

    place(me.core)
    parts.receive()
    for c in step3:
        c.wait()
    place(1 - me.core)
    eye = one_zero(iota((SL, SL), 0) == iota((SL, SL), 1)).astype(bf16)
    sm = nt_dot(eye, features[...])
    sm_out[...] = sm
    flag_out[0, 0] = jnp.max(sm[FLAG : FLAG + 1, :]).astype(i32)
    even = one_zero(iota((SL, D), 1) == 2 * iota((SL, D), 0)).astype(bf16)
    by_device = nn_dot(even, features[...]).astype(bf16)
    spread = one_zero(iota((SL, FF), 0) == UP + iota((SL, FF), 1) % 8).astype(bf16)
    wide = jnp.where(iota((SL, FF), 0) == iota((SL, FF), 1) // 8, nn_dot(by_device, spread), 0.0).astype(bf16)
    up = nn_dot(jnp.ones((16, SL), bf16), wide)[:1]
    for c in range(4):
        sm_out[UP + c : UP + c + 1, :] = up[:, c * D : (c + 1) * D]


def gather(caps, nbins, lengths, visible, dec_grad, tokens, shards, cid):
    dma = pltpu.SemaphoreType.DMA
    s = jax.ShapeDtypeStruct
    return pl.pallas_call(
        functools.partial(gather_kernel, caps, nbins),
        out_shape=(
            s((D, 8 * D), bf16), s((FF, D), bf16), s((SL, D), f32), s((SL, D), f32), s((1, 1), i32),
        ) + part_outs(caps, nbins),
        in_specs=[hbm()] * 14,
        out_specs=(vmem(),) * 4 + (smem(),) + (vmem(),) * 8,
        scratch_shapes=part_scratch(caps, nbins) + [
            pltpu.VMEM((2, 2, 4, 4, 2, 32, D), bf16), pltpu.VMEM((2, SL), f32), pltpu.VMEM((D, SL), bf16),
            dma((16,)), dma((2, 4, 2)), dma((2, 3)), dma((2, 3)), dma((2, 4)), dma((2, 4)), dma((12,)),
        ] + [pltpu.VMEM(a.shape, a.dtype) for a in (lengths, visible) + shards],
        compiler_params=pltpu.CompilerParams(collective_id=cid, has_side_effects=True, vmem_limit_bytes=VMEM_MOST),
        name="gather_and_exchange",
    )(dec_grad, tokens, lengths, visible, *shards)


def encoder_kernel(
    nbins, cnt_ref, x_ref, ge_ref, seg_ref, w_ref, wd_ref, sm_ref, part_ref,
    enc_ref, gt_ref, gs_ref,
    gw_scr, gwd_scr, sums_scr, bup_scr, qkv_scr, gqkv_scr,
):
    nsup = (cnt_ref[0, 0] + 1) // 2
    M = 2 * SL
    gw_scr[...] = jnp.zeros_like(gw_scr)
    gwd_scr[...] = jnp.zeros_like(gwd_scr)
    sums_scr[...] = jnp.zeros_like(sums_scr)
    bup_scr[...] = jnp.zeros_like(bup_scr)

    def clear(s, _):
        enc_ref[pl.ds(pl.multiple_of(s * M, M), M), :] = jnp.zeros((M, D), bf16)
        return 0

    lax.fori_loop(nsup, nbins // 2, clear, 0)

    gain1, gain2 = sm_ref[GAIN : GAIN + 1, :], sm_ref[GAIN + 1 : GAIN + 2, :]
    shift1, shift2 = sm_ref[SHIFT : SHIFT + 1, :], sm_ref[SHIFT + 1 : SHIFT + 2, :]
    bq, bv, bo, bd = (sm_ref[BIAS + k : BIAS + 1 + k, :] for k in range(4))
    seg_lo, seg_hi = seg_ref[0:1, :], seg_ref[1:2, :]
    row = iota((SL, SL), 0).astype(f32)
    head0 = iota((SL, SL), 1) < 64
    zero_b = jnp.zeros((SL, SL), bf16)
    ind2 = jnp.concatenate([one_zero(head0), one_zero(~head0)], axis=0).astype(bf16)
    units = [(h, p) for h in range(2) for p in range(2)]

    def two(a):
        return jnp.concatenate([jnp.where(head0, a, zero_b), jnp.where(head0, zero_b, a)], axis=0)

    def body(s, _):
        here = pl.ds(pl.multiple_of(s * M, M), M)
        x = x_ref[here, :].astype(f32)
        cen = x - jnp.mean(x, axis=1, keepdims=True)
        r1 = lax.rsqrt(jnp.mean(cen * cen, axis=1, keepdims=True) + EPS)
        xh1 = cen * r1
        nf = (xh1 * gain1 + shift1).astype(bf16)
        qkv_scr[:, :D] = (nn_dot(nf, w_ref[:, :D]) + bq).astype(bf16) * jnp.asarray(0.125, bf16)
        qkv_scr[:, D : 2 * D] = nn_dot(nf, w_ref[:, D : 2 * D]).astype(bf16)
        qkv_scr[:, 2 * D : 3 * D] = (nn_dot(nf, w_ref[:, 2 * D : 3 * D]) + bv).astype(bf16)

        def unit(h, p):
            rows = slice(h * SL, (h + 1) * SL)
            return [qkv_scr[rows, k * D + p * SL : k * D + (p + 1) * SL] for k in range(3)]

        segs = []
        for h in range(2):
            at = row + ((2 * s + h) * SL).astype(f32)
            seg = one_zero((at >= seg_lo) & (at < seg_hi))
            out = ((seg - 1.0) * BIG).astype(bf16)
            segs.append((seg.astype(bf16), jnp.concatenate([out, out], axis=0)))
        saved = {}
        for h in range(2):
            qkv = [unit(h, p) for p in range(2)]
            sc = [
                nt_dot(
                    jnp.concatenate([qkv[p][0], segs[h][0]], axis=1),
                    jnp.concatenate([two(qkv[p][1]), segs[h][1]], axis=1),
                )
                for p in range(2)
            ]
            top = [[jnp.max(sc[p][:, g * SL : (g + 1) * SL], axis=1, keepdims=True) for g in range(2)] for p in range(2)]
            e = [
                jnp.concatenate(
                    [jnp.exp(sc[p][:, g * SL : (g + 1) * SL] - top[p][g]) for g in range(2)], axis=1
                ).astype(bf16)
                for p in range(2)
            ]
            y = [nn_dot(e[p], jnp.concatenate([two(qkv[p][2]), ind2], axis=1)) for p in range(2)]
            for p in range(2):
                rinv = 1.0 / y[p][:, SL:]
                saved[h, p] = (e[p], rinv, y[p][:, :SL] * rinv)
        att = jnp.concatenate(
            [jnp.concatenate([saved[h, p][2] for p in range(2)], axis=1) for h in range(2)], axis=0
        ).astype(bf16)
        mixed = x + nn_dot(att, w_ref[:, 3 * D : 4 * D]) + bo
        cen = mixed - jnp.mean(mixed, axis=1, keepdims=True)
        r2 = lax.rsqrt(jnp.mean(cen * cen, axis=1, keepdims=True) + EPS)
        xh2 = cen * r2
        ns = (xh2 * gain2 + shift2).astype(bf16)
        ns_t = ns.T
        ge_b = ge_ref[here, :]
        ge_t = ge_b.T
        ge = ge_b.astype(f32)

        enc = mixed + bd
        gns = jnp.zeros((M, D), f32)
        for c in range(4):
            cs = slice(c * D, (c + 1) * D)
            ws = slice(4 * D + c * D, 5 * D + c * D)
            v = nn_dot(ns, w_ref[:, ws]) + sm_ref[UP + c : UP + c + 1, :]
            vv = v * v
            a = 0.5 * jnp.tanh(v * (vv * (GELU_A * GELU_B) + GELU_A)) + 0.5
            hact = v * a
            dg = a + hact * (1.0 - a) * (vv * (6.0 * GELU_A * GELU_B) + 2.0 * GELU_A)
            hb = hact.astype(bf16)
            enc = enc + nn_dot(hb, wd_ref[cs, :])
            ghb = (nt_dot(ge_b, wd_ref[cs, :]) * dg).astype(bf16)
            bup_scr[:, cs] += fold8(ghb.astype(f32))
            gns = gns + nt_dot(ghb, w_ref[:, ws])
            gw_scr[:, ws] += nn_dot(ns_t, ghb)
            gwd_scr[:, cs] += nn_dot(ge_t, hb)
        enc_ref[here, :] = enc.astype(bf16)

        sums_scr[7] += fold8(ge)
        sums_scr[1] += fold8(gns * xh2)
        sums_scr[3] += fold8(gns)
        eg = gns * gain2
        gmix = ge + r2 * (eg - jnp.mean(eg, axis=1, keepdims=True) - xh2 * jnp.mean(eg * xh2, axis=1, keepdims=True))
        gao = gmix.astype(bf16)
        sums_scr[6] += fold8(gao.astype(f32))
        gw_scr[:, 3 * D : 4 * D] += tn_dot(att, gao)
        gatt = nt_dot(gao, w_ref[:, 3 * D : 4 * D])
        for h in range(2):
            rows = slice(h * SL, (h + 1) * SL)
            qkv = [unit(h, p) for p in range(2)]
            da = [gatt[rows, p * SL : (p + 1) * SL] * saved[h, p][1] for p in range(2)]
            dao = [(da[p] * saved[h, p][2]).astype(bf16) for p in range(2)]
            da = [da[p].astype(bf16) for p in range(2)]
            dp = [
                nt_dot(jnp.concatenate([da[p], dao[p]], axis=1), jnp.concatenate([two(qkv[p][2]), -ind2], axis=1))
                for p in range(2)
            ]
            e = [saved[h, p][0] for p in range(2)]
            gsc = [(e[p].astype(f32) * dp[p]).astype(bf16) for p in range(2)]
            gq = [nn_dot(gsc[p], two(qkv[p][1])) * 0.125 for p in range(2)]
            gk = [tn_dot(gsc[p], qkv[p][0]) for p in range(2)]
            gv = [tn_dot(e[p], da[p]) for p in range(2)]
            for p in range(2):
                lanes = slice(p * SL, (p + 1) * SL)
                gqkv_scr[rows, p * SL : (p + 1) * SL] = gq[p].astype(bf16)
                gqkv_scr[rows, D + p * SL : D + (p + 1) * SL] = jnp.where(head0, gk[p][:SL], gk[p][SL:]).astype(bf16)
                gqkv_scr[rows, 2 * D + p * SL : 2 * D + (p + 1) * SL] = jnp.where(head0, gv[p][:SL], gv[p][SL:]).astype(bf16)
        gqkv = gqkv_scr[...]
        sums_scr[4] += fold8(gqkv[:, :D].astype(f32))
        sums_scr[5] += fold8(gqkv[:, 2 * D :].astype(f32))
        gw_scr[:, : 3 * D] += tn_dot(nf, gqkv)
        gnf = nt_dot(gqkv, w_ref[:, : 3 * D])
        sums_scr[0] += fold8(gnf * xh1)
        sums_scr[2] += fold8(gnf)
        eg = gnf * gain1
        gtok = gmix + r1 * (eg - jnp.mean(eg, axis=1, keepdims=True) - xh1 * jnp.mean(eg * xh1, axis=1, keepdims=True))
        hi = gtok.astype(bf16)
        lo = (gtok - hi.astype(f32)).astype(bf16)
        for h in range(2):
            rows = slice(h * SL, (h + 1) * SL)
            gt_ref[2 * s + h, :SL, :] = hi[rows]
            gt_ref[2 * s + h, SL:, :] = lo[rows]
        return 0

    lax.fori_loop(0, nsup, body, 0)

    fin = [jnp.sum(sums_scr[k], axis=0, keepdims=True) for k in range(8)]
    gsm = jnp.concatenate(
        [part_ref[:GAIN, :]] + fin + [part_ref[MASK : MASK + 1, :], jnp.zeros((SL - MASK - 1, D), f32)], axis=0
    ).astype(bf16)
    eye = one_zero(iota((D, D), 0) == iota((D, D), 1)).astype(bf16)
    smt = nt_dot(eye, gsm)
    bup = jnp.sum(bup_scr[...], axis=0, keepdims=True).astype(bf16)
    dsel = iota((SL, FF), 0) == iota((SL, FF), 1) // 8
    bup_m = jnp.where(dsel, jnp.broadcast_to(bup, (SL, FF)), jnp.zeros((SL, FF), bf16))
    rep = one_zero(iota((SL, FF), 0) == UP + iota((SL, FF), 1) % 8).astype(bf16)
    bup_d = nt_dot(bup_m, rep)
    even = one_zero(iota((D, SL), 0) == 2 * iota((D, SL), 1)).astype(bf16)
    smt = (smt + nn_dot(even, bup_d.astype(bf16))).astype(bf16)
    gwd_t = [nt_dot(eye, gwd_scr[:, c * D : (c + 1) * D].astype(bf16)).astype(bf16) for c in range(4)]
    pr, pc = iota((D, D), 0), iota((D, D), 1)
    pd, prr = pr // 32, pr % 32
    want = jnp.where(prr < 18, (prr % 9) * 16 + pd * 2 + prr // 9, jnp.where(prr < 26, 144 + pd * 8 + prr - 18, -1))
    perm = one_zero(want == pc).astype(bf16)
    sm_pad = jnp.zeros((16, SL), bf16)
    tail = jnp.zeros((48, D), bf16)
    for qn in range(16):
        r16 = slice(qn * 16, qn * 16 + 16)
        parts = [gw_scr[r16, bb * D : (bb + 1) * D].astype(bf16) for bb in range(8)]
        parts.append(jnp.concatenate([smt[r16], sm_pad], axis=1))
        o = (qn % 4) * 64
        parts.append(gwd_t[qn // 4][o : o + 64])
        parts.append(tail)
        gs_ref[qn] = nn_dot(perm, jnp.concatenate(parts, axis=0)).astype(bf16)


def encoder(nbins, cnt, x, ge, seg, w, wd, sm, part):
    return pl.pallas_call(
        functools.partial(encoder_kernel, nbins),
        out_shape=(
            jax.ShapeDtypeStruct((nbins * SL, D), bf16),
            jax.ShapeDtypeStruct((nbins, 2 * SL, D), bf16),
            jax.ShapeDtypeStruct((16, D, D), bf16),
        ),
        in_specs=[pl.BlockSpec(memory_space=pltpu.SMEM)] + [vmem()] * 7,
        out_specs=(vmem(),) * 3,
        scratch_shapes=[
            pltpu.VMEM((D, 2048), f32), pltpu.VMEM((D, FF), f32), pltpu.VMEM((8, 8, D), f32), pltpu.VMEM((8, FF), f32),
            pltpu.VMEM((2 * SL, 3 * D), bf16), pltpu.VMEM((2 * SL, 3 * D), bf16),
        ],
        compiler_params=pltpu.CompilerParams(vmem_limit_bytes=VMEM_LIMIT),
        name="encoder_fwd_bwd",
    )(cnt, x, ge, seg, w, wd, sm, part)


def pack_encoded(caps, nbins, enc_ref, src_ref, s_scr):
    total = sum(caps)
    row = iota((256, SL), 0).astype(f32)
    for c in range(0, total, 256):
        wide = min(256, total - c)

        def one(b, acc):
            src = src_ref[pl.ds(pl.multiple_of(b * 16, 16), 16), :]
            hit = [one_zero(row[:wide] + float(c + 1) == src[8 * k : 8 * k + 1]) for k in range(2)]
            rows = enc_ref[pl.ds(pl.multiple_of(b * 256, 256), 256), :]
            return acc + nn_dot(jnp.concatenate(hit, axis=1).astype(bf16), rows)

        s_scr[c : c + wide, :] = lax.fori_loop(0, nbins // 2, one, jnp.zeros((wide, D), f32)).astype(bf16)


def scatter_kernel(
    caps, nbins, bins_ref, gs_ref, enc_ref, src_ref, gt_ref, slot_ref, cols_ref, sm_ref,
    dec_out, gtok_out, slab_out,
    got1, sum1, got2, sum2, got3, s_scr, rows_scr, s_sem, r_sem, s1, r1, s2, r2, s3, r3, own_sem,
):
    me = Place()
    base = bases(caps)
    most, room = decode_room(caps)
    steps = sm_ref[pl.ds(pl.multiple_of(TE + 8 * me.seq, 8), 8), :]
    extra = jnp.concatenate([sm_ref[MASK : MASK + 1, :], steps, jnp.zeros((room - most - 9, D), f32)], axis=0).astype(bf16)
    for i in range(8):
        rows_scr[i, :most] = jnp.zeros((most, D), bf16)
        rows_scr[i, most:] = extra
    barrier, count = me.greet()
    pl.semaphore_wait(barrier, count)

    step1 = []
    for x in (0, 2, 1, 3):
        c = remote(gs_ref.at[x, 1 - me.core], got1.at[x], s1.at[x], r1.at[x], me.sibling())
        c.start()
        step1.append((x, c))
    pack_encoded(caps, nbins, enc_ref, src_ref, s_scr)
    for j in range(8):
        part = s_scr.at[pl.ds(base[j], caps[j])]
        there = rows_scr.at[me.seq, pl.ds(0, caps[j])]

        @pl.when(me.seq == j)
        def _():
            pltpu.make_async_copy(part, there, own_sem).start()

        @pl.when(me.seq != j)
        def _():
            remote(part, there, s_sem.at[j], r_sem.at[me.seq], (j, me.dp)).start()

    def unpack(first, last):
        lane = iota((SL, SL), 1).astype(f32)
        for t in range(first, last):
            hit = one_zero(slot_ref[:, t : t + 1] == lane).astype(bf16)
            gtok_out[t] = nn_dot(jnp.concatenate([hit, hit], axis=1), gt_ref[bins_ref[0, t]])

    unpack(0, 8)
    for x, c in step1:
        c.wait()
        for z in range(4):
            for y in range(4):
                total = gs_ref[x, me.core, 4 * z + y].astype(f32) + got1[x, 4 * z + y].astype(f32)
                if x < 2:
                    sum1[0, z, x % 2, y] = total.astype(bf16)
                else:
                    sum1[1, y, x % 2, z] = total.astype(bf16)
    first = (me.z, me.y)
    second = (me.y, me.z)
    peers = (me.z_peer, me.y_peer)
    step2 = []
    for k in (2, 1, 3):
        for h in range(2):
            c = remote(sum1.at[h, (first[h] + k) % 4], got2.at[h, k - 1], s2.at[h, k - 1], r2.at[h, k - 1], peers[h](k))
            c.start()
            step2.append(c)
    unpack(8, NT)
    for c in step2:
        c.wait()
    for h in range(2):
        for x2 in range(2):
            for o in range(4):
                total = sum1[h, first[h], x2, o].astype(f32)
                for k in range(3):
                    total = total + got2[h, k, x2, o].astype(f32)
                sum2[h, x2, o] = total.astype(bf16)

    half = me.x // 2
    mine = second[0] + half * (second[1] - second[0])
    for h in range(2):
        for x2 in range(2):
            for o in range(4):
                is_me = (me.x == 2 * h + x2) & (second[h] == o)
                peer = me.at(2 * h + x2, o if h == 0 else me.y, me.z if h == 0 else o)

                @pl.when(is_me)
                def _():
                    got3[o, 2 * h + x2] = sum2[h, x2, o]

                @pl.when(jnp.logical_not(is_me))
                def _():
                    remote(
                        sum2.at[h, x2, o], got3.at[second[h], me.x], s3.at[h, x2, o], r3.at[second[h], me.x], peer
                    ).start()

    lane = iota((PART, SL), 1).astype(f32)
    cols = cols_ref[...]
    for j in range(8):
        @pl.when(me.seq == j)
        def _():
            here = rows_scr.at[0, pl.ds(0, caps[j])]
            for i in range(8):
                if i != j:
                    arrived(here, r_sem.at[i])
            arrived(here, own_sem)

        @pl.when(me.seq != j)
        def _():
            arrived(s_scr.at[pl.ds(base[j], caps[j])], s_sem.at[j])
    for i in range(8):
        hit = []
        for c in range(0, room, SL):
            one = cols[:, i : i + 1] == lane + float(c)
            if c + SL > most:
                one = one | (cols[:, 8 + i : 9 + i] == lane + float(c))
            hit.append(one_zero(one))
        got = nn_dot(jnp.concatenate(hit, axis=1).astype(bf16), rows_scr[i]).astype(bf16)
        dec_out[:, 8 * i : 8 * i + 8] = got.reshape(MICRO, 8, 16, D)

    for o in range(4):
        for x in range(4):
            is_me = (me.x == x) & (mine == o)

            @pl.when(jnp.logical_not(is_me))
            def _():
                arrived(got3.at[o, x], r3.at[o, x])
    for h in range(2):
        for x2 in range(2):
            for o in range(4):
                is_me = (me.x == 2 * h + x2) & (second[h] == o)

                @pl.when(jnp.logical_not(is_me))
                def _():
                    arrived(sum2.at[h, x2, o], s3.at[h, x2, o])
    slab = jnp.zeros((32, D), f32)
    for o in range(4):
        for x in range(4):
            slab = slab + got3[o, x].astype(f32)

    slab_out[...] = slab


def scatter(caps, nbins, bins, gs, enc, src, gt, slot, cols, sm, cid):
    dma = pltpu.SemaphoreType.DMA
    most, room = decode_room(caps)
    s = jax.ShapeDtypeStruct
    return pl.pallas_call(
        functools.partial(scatter_kernel, caps, nbins),
        out_shape=(
            s((MICRO, TRAJ, 16, D), bf16), s((NT, SL, D), f32), s((32, D), f32),
        ),
        in_specs=[smem()] + [vmem()] * 7,
        out_specs=(vmem(),) * 3,
        scratch_shapes=[
            pltpu.VMEM((4, 16, 32, D), bf16), pltpu.VMEM((2, 4, 2, 4, 32, D), bf16),
            pltpu.VMEM((2, 3, 2, 4, 32, D), bf16), pltpu.VMEM((2, 2, 4, 32, D), bf16),
            pltpu.VMEM((4, 4, 32, D), bf16), pltpu.VMEM((sum(caps), D), bf16), pltpu.VMEM((8, room, D), bf16),
            dma((8,)), dma((8,)), dma((4,)), dma((4,)), dma((2, 3)), dma((2, 3)), dma((2, 2, 4)), dma((4, 4)), dma,
        ],
        compiler_params=pltpu.CompilerParams(collective_id=cid, has_side_effects=True, vmem_limit_bytes=VMEM_LIMIT),
        name="scatter_and_exchange",
    )(bins, gs, enc, src, gt, slot, cols, sm)


def finish_kernel(
    dec_ref, gtok_ref, slab_ref,
    dec_out, gtok_out, gain_out, shift_out, wq_out, wo_out, wu_out, wd_out, bias_out, up_out, mask_out, te_out, sems,
):
    copies = [
        pltpu.make_async_copy(dec_ref, dec_out, sems.at[0]), pltpu.make_async_copy(gtok_ref, gtok_out, sems.at[1])
    ]
    for c in copies:
        c.start()
    slab = slab_ref[...]
    for f in range(2):
        one = slice(f, f + 1)
        for b in range(3):
            wq_out[one, b * D : (b + 1) * D] = slab[9 * f + b : 9 * f + b + 1]
        wo_out[one, :] = slab[9 * f + 3 : 9 * f + 4]
        for b in range(4):
            wu_out[one, b * D : (b + 1) * D] = slab[9 * f + 4 + b : 9 * f + 5 + b]
        row = slab[9 * f + 8 : 9 * f + 9]
        te_out[one, :] = row[:, TE : TE + 64]
        bias_out[one, :] = row[:, BIAS : BIAS + 4]
        mask_out[:, one] = row[:, MASK : MASK + 1]
        for g in range(2):
            gain_out[g : g + 1, one] = row[:, GAIN + g : GAIN + g + 1]
            shift_out[g : g + 1, one] = row[:, SHIFT + g : SHIFT + g + 1]
    wd_out[...] = slab[18:26]
    up_out[...] = slab[8:9, UP : UP + 8]
    for c in copies:
        c.wait()


def finish(dec, gtok, slab):
    s = jax.ShapeDtypeStruct
    return pl.pallas_call(
        finish_kernel,
        out_shape=(
            s(dec.shape, dec.dtype), s(gtok.shape, gtok.dtype), s((2, 2), f32), s((2, 2), f32), s((2, 3 * D), f32),
            s((2, D), f32), s((2, FF), f32), s((8, D), f32), s((2, 4), f32), s((1, 8), f32), s((1, 2), f32),
            s((2, 64), f32),
        ),
        in_specs=[vmem()] * 3,
        out_specs=(hbm(),) * 2 + (vmem(),) * 10,
        scratch_shapes=[pltpu.SemaphoreType.DMA((2,))],
        compiler_params=pltpu.CompilerParams(vmem_limit_bytes=VMEM_LIMIT),
        name="results",
    )(dec, gtok, slab)


def per_device(
    tokens, lengths, visible, norm_gains, norm_biases, w_qkv, w_out, w_up, w_down, proj_biases, up_bias, mask_token,
    time_embed, dec_grad,
):
    lengths, visible = lengths[:, 0], visible[:, 0]
    tok = tokens.reshape(NT, SL, D)
    dg = dec_grad[:, 0]
    shards = (
        w_qkv, w_out, w_up, w_down, norm_gains, norm_biases, proj_biases.T, up_bias[None], mask_token[None], time_embed.T
    )
    w, wd, sm, part, flag, *packed = gather(CAPS, NBINS, lengths, visible, dg, tok, shards, 0)

    def rest(caps, nbins, packed, cid):
        x, ge, seg, src, slot, bins, count, cols = packed
        enc, gt, gs = encoder(nbins, count, x, ge, seg, w, wd, sm, part)
        out = scatter(caps, nbins, bins, gs.reshape(4, 2, 16, 32, D), enc, src, gt, slot, cols, sm, cid)
        return tuple(finish(*out))

    def roomy():
        return rest(FULL, NFULL, exchange(FULL, NFULL, lengths, visible, dg, tok, 1), 2)

    outs = lax.cond(flag[0, 0] > 0, roomy, lambda: rest(CAPS, NBINS, packed, 3))
    dec, gtok, gain, shift, wq, wo, wu, wdn, bias, up, mask, te = outs
    return (
        dec.reshape(MICRO, 1, TRAJ, 16, D), gtok.reshape(MICRO, 1, 8, SL, D), gain, shift, wq, wo, wu, wdn, bias.T,
        up.reshape(8), mask.reshape(2), te.T,
    )


def solution(mesh):
    everyone = ("seq", "dp")
    return jax.shard_map(
        per_device,
        mesh=mesh,
        in_specs=(
            P(None, "dp", "seq", None, None), P(None, "dp", None), P(None, "dp", None, None), P(None, everyone),
            P(None, everyone), P(everyone, None), P(everyone, None), P(everyone, None), P(everyone, None),
            P(None, everyone), P(everyone), P(everyone), P(None, everyone), P(None, "dp", None, "seq", None),
        ),
        out_specs=(
            P(None, "dp", None, "seq", None), P(None, "dp", "seq", None, None), P(None, everyone), P(None, everyone),
            P(everyone, None), P(everyone, None), P(everyone, None), P(everyone, None), P(None, everyone), P(everyone),
            P(everyone), P(None, everyone),
        ),
        check_vma=False,
    )
```

time: 113 us -> 75.2 us (0.67)
  Pallas kernels: 101 us -> 71.9 us
  local copies, waits for them, and re-layouts: 7.08 us -> 0.02 us
    pallas_call x4, Pallas kernels: 101 us -> 71.9 us  [the longest x1 28.9 us: scatter(): pl.pallas_call(functools.partial(scatter_kernel, caps, nbins), out_shape=...]
    unnamed x8, local copies, waits for them, and re-layouts: 4.39 us -> 0.02 us
    concatenate x2 -> x0, local copies, waits for them, and re-layouts: 1.93 us -> none  [the longest x1 1.27 us: per_device(): small = jnp.concatenate([small, ups, jnp.zeros((2, 40), bf16)], axis=1)]
where the time goes in v2:
time: 75.2 us; the launch traced here: 74 us
  Pallas kernels  71.9 us (96%)
  between operations  1.5 us (2%)
    pallas_call x1, Pallas kernels, scatter(): pl.pallas_call(functools.partial(scatter_kernel, caps, nbins), out_shape=...  28.9 us
    pallas_call x1, Pallas kernels, gather(): pl.pallas_call(functools.partial(gather_kernel, caps, nbins), out_shape=(...  25.5 us
    pallas_call x1, Pallas kernels, encoder(): pl.pallas_call(functools.partial(encoder_kernel, nbins), out_shape=(jax.S...  14.1 us
    pallas_call x1, Pallas kernels, finish(): pl.pallas_call(finish_kernel, out_shape=(s(dec.shape, dec.dtype), s(gtok....  3.36 us

profile of v2, /device:TPU:0, one launch (start us, length us, event | category | flops | bytes accessed | tf_op | source)
XLA Modules:
  0.0 74.0 jit_solution(1371254278248311133)
XLA Ops:
  0.6 0.0 copy-start
  0.7 0.0 copy-start.1
  0.7 0.0 copy-start.2
  0.7 0.0 copy-start.3
  0.7 25.5 %gather_and_exchange.1 = (bf16[256,2048]{1,0:T(8,128)(2,1)S(1)}, bf16[1024,256]{1,0:T(8,128)(2,1)S(1)}, f32[128,256]{1,0:T(8,128)S(1)}, f32[128,256]{1,0:T(8,128...) custom-call(bf16[4,64,16,256]{3,2,1,0:T(8,128)(2,1)} %bitcast.25, ...), custom_call_target="tpu_custom_call" | custom-call | tf_op jit(solution)/shard_map/gather_and_exchange/pallas_call | solution.py:558
  26.8 0.0 copy-done
  26.8 0.0 copy-done.1
  26.8 0.0 copy-done.2
  26.8 0.0 copy-done.3
  26.8 46.9 %conditional.1 = ((bf16[4,64,16,256]{3,2,1,0:T(8,128)(2,1)}, f32[32,128,256]{2,1,0:T(8,128)}, f32[2,2]{1,0:T(2,128)}, f32[2,2]{1,0:T(2,128)}, f32[2,768]{1,0:T(2...) conditional(s32[]{:T(128)} %bitcast.10, ...), branch_computations={%region_0.0_spmd.clone, %region_1.0_spmd.clone} | conditional | bytes 8 | solution.py:1016
  26.8 14.1 %encoder_fwd_bwd.2 = (bf16[1024,256]{1,0:T(8,128)(2,1)S(1)}, bf16[8,256,256]{2,1,0:T(8,128)(2,1)S(1)}, bf16[16,256,256]{2,1,0:T(8,128)(2,1)S(1)}) custom-call(s32[8,128]{1,0:T(8,128)S(1)} %get-tuple-element.221.cnt_ref, bf16[1024,256]{1,0:T(8,128)(2,1)S(1)} %get-tuple-element.222.x_ref, bf16[1024,256]{1,0:T(8,128)(2,1)S(1)} %get-tuple-element.223.ge_ref, ...), custom_call_target="tpu_custom_call" | custom-call | tf_op jit(solution)/shard_map/cond/branch_0_fun/encoder_fwd_bwd/pallas_call | solution.py:758
  40.9 28.9 %scatter_and_exchange.2 = (bf16[4,64,16,256]{3,2,1,0:T(8,128)(2,1)S(1)}, f32[32,128,256]{2,1,0:T(8,128)S(1)}, f32[32,256]{1,0:T(8,128)S(1)}) custom-call(s32[8,128]{1,0:T(8,128)S(1)} %get-tuple-element.220.bins_ref, bf16[4,2,16,32,256]{4,3,2,1,0:T(8,128)(2,1)S(1)} %bitcast.23, bf16[1024,256]{1,0:T(8,128)(2,1)S(1)} %get-tuple-element.230.enc_ref, ...), custom_call_target="tpu_custom_call" | custom-call | tf_op jit(solution)/shard_map/cond/branch_0_fun/scatter_and_exchange/pallas_call | solution.py:930
  69.8 3.4 %results.2 = (bf16[4,64,16,256]{3,2,1,0:T(8,128)(2,1)}, f32[32,128,256]{2,1,0:T(8,128)}, f32[2,2]{1,0:T(2,128)}, f32[2,2]{1,0:T(2,128)}, f32[2,768]{1,0:T(2,128)...) custom-call(bf16[4,64,16,256]{3,2,1,0:T(8,128)(2,1)S(1)} %get-tuple-, ...), custom_call_target="tpu_custom_call" | custom-call | tf_op jit(solution)/shard_map/cond/branch_0_fun/results/pallas_call | solution.py:980
Async XLA Ops:
  0.6 26.1 %copy-start = (bf16[4,1,64,16,256]{4,3,2,1,0:T(8,128)(2,1)S(1)}, bf16[4,1,64,16,256]{4,3,2,1,0:T(8,128)(2,1)}, u32[]{:S(2)}) copy-start(bf16[4,1,64,16,256]{4,3,2,1,0:T(8,128)(2,1)} %param.29) | copy-start | bytes 6291460
  0.7 26.1 %copy-start.1 = (bf16[4,1,8,128,256]{4,3,2,1,0:T(8,128)(2,1)S(1)}, bf16[4,1,8,128,256]{4,3,2,1,0:T(8,128)(2,1)}, u32[]{:S(2)}) copy-start(bf16[4,1,8,128,256]{4,3,2,1,0:T(8,128)(2,1)} %param.16) | copy-start | bytes 6291460
  0.7 26.1 %copy-start.2 = (s32[4,1,64,128]{3,2,1,0:T(8,128)S(1)}, s32[4,1,64,128]{3,2,1,0:T(8,128)}, u32[]{:S(2)}) copy-start(s32[4,1,64,128]{3,2,1,0:T(8,128)} %param.18) | copy-start | bytes 393220
  0.7 26.1 %copy-start.3 = (s32[4,1,64]{2,1,0:T(1,128)S(1)}, s32[4,1,64]{2,1,0:T(1,128)}, u32[]{:S(2)}) copy-start(s32[4,1,64]{2,1,0:T(1,128)} %param.17) | copy-start | bytes 3076
